TPU v7x, 32 devices: a whole 2x2x4 slice. The times are simulated.
32 devices in a mesh: tower: 2 (over core), batch: 16 (over z, y, x).
Axes of the slice: x: 2, y: 2, z: 4, core: 2. Of those that a mesh axis runs over, the one named last changes fastest.
Arguments:
- states: bfloat16 [2, 96, 256, 768], P('tower', 'batch'), may hold values from -6 to 6
- q_lengths: int32 [96, 4], P('batch'), may hold values from 1 to 64, as said below
- dataset_ids: int32 [96], replicated, may hold values from 0 to 3
- positives: int32 [384], P('batch'), may hold values from 0 to 95
- w_qkv: bfloat16 [2, 768, 2304], P('tower', 'batch'), may hold values from -0.21875 to 0.21875
- w_out: bfloat16 [2, 768, 768], P('tower', 'batch'), may hold values from -1.75 to 1.75
- w_in: bfloat16 [2, 768, 3072], P('tower', 'batch'), may hold values from -0.21875 to 0.21875
- w_back: bfloat16 [2, 3072, 768], P('tower', 'batch'), may hold values from -0.109375 to 0.109375
- gain_first: bfloat16 [2, 768], P('tower', 'batch'), may hold values from 0.5 to 1.5
- bias_first: bfloat16 [2, 768], P('tower', 'batch'), may hold values from -1.5 to 1.5
- gain_second: bfloat16 [2, 768], P('tower', 'batch'), may hold values from 0.5 to 1.5
- bias_second: bfloat16 [2, 768], P('tower', 'batch'), may hold values from -1.5 to 1.5
Outputs:
- loss: float32 [], replicated
- encoded: bfloat16 [2, 96, 256, 768], P('tower', 'batch')
- states_grad: float32 [2, 96, 256, 768], P('tower', 'batch')
- grad_qkv: float32 [2, 768, 2304], P('tower', 'batch')
- grad_out: float32 [2, 768, 768], P('tower', 'batch')
- grad_in: float32 [2, 768, 3072], P('tower', 'batch')
- grad_back: float32 [2, 3072, 768], P('tower', 'batch')
- grad_gain_first: float32 [2, 768], P('tower', 'batch')
- grad_bias_first: float32 [2, 768], P('tower', 'batch')
- grad_gain_second: float32 [2, 768], P('tower', 'batch')
- grad_bias_second: float32 [2, 768], P('tower', 'batch')
Inputs may be any that keep to these rules, and one draw needn't show every extreme that they name: `q_lengths`: every row of 4 questions holds one question of length 64.
All inputs are finite; a program needn't handle non-finite values.
Results may differ from a plain program's by a relative error of at most 0.017.
Values may be sent and summed in bfloat16 or wider, within the bound.
No kernel may reach another device: no remote copies, remote signals or barrier semaphores. Data moves between devices by JAX's collectives and lax.ppermute only.
A program may use at most 192 MiB of HBM per device.

v0:
```python
import math

import jax
import jax.numpy as jnp
from jax import lax
from jax.sharding import PartitionSpec as P

D = 768
HEADS = 12
HEAD = 64
SEQ_LEN = 256
QLEN = 64
MICRO = 3
SLOTS = 4


exact_mode = lax.Precision.HIGHEST


def norm_rows(summed, gain, shift):
    center = summed - jnp.mean(summed, axis=-1, keepdims=True)
    spread = jnp.mean(center * center, axis=-1, keepdims=True)
    return center * lax.rsqrt(spread + 1e-05) * gain + shift


def gelu_exact(values):
    return jax.nn.gelu(values, approximate=False)


def key_valid(lengths, asking):
    position = jnp.arange(SEQ_LEN, dtype=jnp.int32)
    slot_of = position // QLEN
    within = position % QLEN
    hit = slot_of[None, :] == jnp.arange(SLOTS, dtype=jnp.int32)[:, None]
    limit = jnp.sum(jnp.where(hit[None], lengths[:, :, None], 0), axis=1)
    open_key = within[None] < limit
    same_slot = slot_of[:, None] == slot_of[None]
    return same_slot[None] & open_key[:, None, :] | jnp.logical_not(asking)


def unpack(gathered):
    matrices = tuple((item[0] for item in gathered[:4]))
    norms = tuple((item[0].astype(jnp.float32) for item in gathered[4:]))
    return matrices + norms


def attend(query, keyset, valset, valid):
    score = jnp.einsum("rqhe,rkhe->rhqk", query, keyset, preferred_element_type=jnp.float32) * (
        1.0 / math.sqrt(HEAD)
    )
    score = jnp.where(valid[:, None], score, -1000000000.0)
    highest = jnp.max(score, axis=-1, keepdims=True)
    expo = jnp.exp(score - highest)
    probs = expo / jnp.sum(expo, axis=-1, keepdims=True)
    weights_low = probs.astype(jnp.bfloat16)
    context = jnp.einsum(
        "rhqk,rkhe->rqhe", weights_low, valset, preferred_element_type=jnp.float32
    ).astype(jnp.bfloat16)
    return (probs, weights_low, context)


def encode(inputs, weights, valid):
    w_mix, w_proj, w_up, w_down, gain_one, shift_one, gain_two, shift_two = weights
    count = inputs.shape[0]
    mixed = jnp.einsum("rld,de->rle", inputs, w_mix, preferred_element_type=jnp.float32).astype(
        jnp.bfloat16
    )
    query = mixed[..., :D].reshape(count, SEQ_LEN, HEADS, HEAD)
    keyset = mixed[..., D : 2 * D].reshape(count, SEQ_LEN, HEADS, HEAD)
    valset = mixed[..., 2 * D :].reshape(count, SEQ_LEN, HEADS, HEAD)
    probs, weights_low, context = attend(query, keyset, valset, valid)
    attended = jnp.einsum(
        "rld,de->rle",
        context.reshape(count, SEQ_LEN, D),
        w_proj,
        preferred_element_type=jnp.float32,
    )
    first = norm_rows(inputs.astype(jnp.float32) + attended, gain_one, shift_one)
    upward = jnp.einsum(
        "rld,df->rlf", first.astype(jnp.bfloat16), w_up, preferred_element_type=jnp.float32
    )
    active = gelu_exact(upward).astype(jnp.bfloat16)
    downward = jnp.einsum("rlf,fd->rld", active, w_down, preferred_element_type=jnp.float32)
    return norm_rows(first + downward, gain_two, shift_two)


def body(
    states,
    q_lengths,
    dataset_ids,
    positives,
    w_qkv,
    w_out,
    w_in,
    w_back,
    gain_first,
    bias_first,
    gain_second,
    bias_second,
):
    asking = lax.axis_index("tower") == 0
    rows_all = states.shape[1]
    per_step = rows_all // MICRO
    valid_all = key_valid(q_lengths, asking)
    encoded_parts = []
    head_parts = []
    for micro_step in range(MICRO):
        weights = unpack(
            (
                lax.all_gather(w_qkv, "batch", axis=1, tiled=True),
                lax.all_gather(w_out, "batch", axis=1, tiled=True),
                lax.all_gather(w_in, "batch", axis=1, tiled=True),
                lax.all_gather(w_back, "batch", axis=1, tiled=True),
                lax.all_gather(gain_first, "batch", axis=1, tiled=True),
                lax.all_gather(bias_first, "batch", axis=1, tiled=True),
                lax.all_gather(gain_second, "batch", axis=1, tiled=True),
                lax.all_gather(bias_second, "batch", axis=1, tiled=True),
            )
        )
        lower = micro_step * per_step
        final = encode(
            states[0, lower : lower + per_step], weights, valid_all[lower : lower + per_step]
        )
        encoded_parts.append(final.astype(jnp.bfloat16))
        head_parts.append(final.reshape(per_step, SLOTS, QLEN, D)[:, :, 0].astype(jnp.bfloat16))
    encoded = jnp.concatenate(encoded_parts)[None]
    all_heads = jnp.concatenate(head_parts)
    own_heads = all_heads[:, 0]
    everyone = lax.all_gather(own_heads, ("tower", "batch"), axis=0, tiled=True)
    passage_heads = everyone[everyone.shape[0] // 2 :]
    asked = all_heads.reshape(rows_all * SLOTS, D)
    logit_scale = 2.0 / math.sqrt(D)
    logits = (
        jnp.einsum("qd,pd->qp", asked, passage_heads, preferred_element_type=jnp.float32)
        * logit_scale
    )
    passage_count = passage_heads.shape[0]
    chosen = positives[:, None] == jnp.arange(passage_count, dtype=jnp.int32)[None]
    asked_data = jnp.sum(jnp.where(chosen, dataset_ids[None], 0), axis=1)
    same_data = asked_data[:, None] == dataset_ids[None]
    masked = jnp.where(same_data, logits, -1000000000.0)
    highest = jnp.max(masked, axis=1, keepdims=True)
    expo = jnp.exp(masked - highest)
    total_exp = jnp.sum(expo, axis=1, keepdims=True)
    log_total = highest[:, 0] + jnp.log(total_exp[:, 0])
    target = jnp.sum(jnp.where(chosen, logits, 0.0), axis=1)
    question_total = asked.shape[0] * lax.axis_size("batch")
    asking_weight = asking.astype(jnp.float32)
    loss_share = asking_weight * jnp.sum(log_total - target) / question_total
    loss_value = lax.psum(loss_share, ("tower", "batch"))
    d_logits = (
        asking_weight
        * (expo / total_exp - chosen.astype(jnp.float32))
        / question_total
        * logit_scale
    )
    d_asked = jnp.dot(d_logits, passage_heads.astype(jnp.float32), precision=exact_mode)
    d_passages = jnp.dot(d_logits.T, asked.astype(jnp.float32), precision=exact_mode)
    own_grad = lax.psum_scatter(
        jnp.concatenate([jnp.zeros_like(d_passages), d_passages]),
        ("tower", "batch"),
        scatter_dimension=0,
        tiled=True,
    )
    passage_grad = jnp.concatenate(
        [own_grad[:, None], jnp.zeros((rows_all, SLOTS - 1, D), jnp.float32)], axis=1
    )
    d_heads = jnp.where(asking, d_asked.reshape(rows_all, SLOTS, D), passage_grad)
    totals = None
    grad_parts = []
    for micro_step in range(MICRO):
        weights = unpack(
            (
                lax.all_gather(w_qkv, "batch", axis=1, tiled=True),
                lax.all_gather(w_out, "batch", axis=1, tiled=True),
                lax.all_gather(w_in, "batch", axis=1, tiled=True),
                lax.all_gather(w_back, "batch", axis=1, tiled=True),
                lax.all_gather(gain_first, "batch", axis=1, tiled=True),
                lax.all_gather(bias_first, "batch", axis=1, tiled=True),
                lax.all_gather(gain_second, "batch", axis=1, tiled=True),
                lax.all_gather(bias_second, "batch", axis=1, tiled=True),
            )
        )
        w_mix, w_proj, w_up, w_down, gain_one, shift_one, gain_two, shift_two = weights
        lower = micro_step * per_step
        inputs = states[0, lower : lower + per_step]
        valid = valid_all[lower : lower + per_step]
        d_top = d_heads[lower : lower + per_step]
        keyval = jnp.einsum(
            "rld,de->rle", inputs, w_mix[:, D:], preferred_element_type=jnp.float32
        ).astype(jnp.bfloat16)
        keyset = keyval[..., :D].reshape(per_step, SEQ_LEN, HEADS, HEAD)
        valset = keyval[..., D:].reshape(per_step, SEQ_LEN, HEADS, HEAD)
        picked = inputs.reshape(per_step, SLOTS, QLEN, D)[:, :, 0]
        query_flat = jnp.einsum(
            "rsd,de->rse", picked, w_mix[:, :D], preferred_element_type=jnp.float32
        ).astype(jnp.bfloat16)
        query = query_flat.reshape(per_step, SLOTS, HEADS, HEAD)
        valid_pick = valid.reshape(per_step, SLOTS, QLEN, SEQ_LEN)[:, :, 0]
        probs, weights_low, context = attend(query, keyset, valset, valid_pick)
        flat_context = context.reshape(per_step, SLOTS, D)
        attended = jnp.einsum(
            "rsd,de->rse", flat_context, w_proj, preferred_element_type=jnp.float32
        )
        first, first_back = jax.vjp(
            norm_rows, picked.astype(jnp.float32) + attended, gain_one, shift_one
        )
        first_low = first.astype(jnp.bfloat16)
        upward = jnp.einsum("rsd,df->rsf", first_low, w_up, preferred_element_type=jnp.float32)
        active_full, active_back = jax.vjp(gelu_exact, upward)
        active = active_full.astype(jnp.bfloat16)
        downward = jnp.einsum("rsf,fd->rsd", active, w_down, preferred_element_type=jnp.float32)
        unused_final, final_back = jax.vjp(norm_rows, first + downward, gain_two, shift_two)
        d_second, d_gain_two, d_shift_two = final_back(d_top)
        d_down = d_second.astype(jnp.bfloat16)
        step_down = jnp.einsum("rsf,rsd->fd", active, d_down, preferred_element_type=jnp.float32)
        d_active = jnp.einsum("rsd,fd->rsf", d_down, w_down, preferred_element_type=jnp.float32)
        d_up = active_back(d_active)[0].astype(jnp.bfloat16)
        step_up = jnp.einsum("rsd,rsf->df", first_low, d_up, preferred_element_type=jnp.float32)
        d_first = d_second + jnp.einsum(
            "rsf,df->rsd", d_up, w_up, preferred_element_type=jnp.float32
        )
        d_sum, d_gain_one, d_shift_one = first_back(d_first)
        d_attended = d_sum.astype(jnp.bfloat16)
        step_proj = jnp.einsum(
            "rsc,rsd->cd", flat_context, d_attended, preferred_element_type=jnp.float32
        )
        d_context = jnp.einsum(
            "rsd,cd->rsc", d_attended, w_proj, preferred_element_type=jnp.float32
        ).astype(jnp.bfloat16)
        d_context = d_context.reshape(per_step, SLOTS, HEADS, HEAD)
        d_probs = jnp.einsum(
            "rqhe,rkhe->rhqk", d_context, valset, preferred_element_type=jnp.float32
        )
        d_score = (probs * (d_probs - jnp.sum(d_probs * probs, axis=-1, keepdims=True))).astype(
            jnp.bfloat16
        )
        head_scale = 1.0 / math.sqrt(HEAD)
        d_query = (
            jnp.einsum("rhqk,rkhe->rqhe", d_score, keyset, preferred_element_type=jnp.float32)
            * head_scale
        ).astype(jnp.bfloat16)
        d_keys = (
            jnp.einsum("rhqk,rqhe->rkhe", d_score, query, preferred_element_type=jnp.float32)
            * head_scale
        ).astype(jnp.bfloat16)
        d_values = jnp.einsum(
            "rhqk,rqhe->rkhe", weights_low, d_context, preferred_element_type=jnp.float32
        ).astype(jnp.bfloat16)
        d_query = d_query.reshape(per_step, SLOTS, D)
        d_keyval = jnp.concatenate(
            [d_keys.reshape(per_step, SEQ_LEN, D), d_values.reshape(per_step, SEQ_LEN, D)], axis=-1
        )
        step_query = jnp.einsum("rsd,rse->de", picked, d_query, preferred_element_type=jnp.float32)
        step_keyval = jnp.einsum(
            "rld,rle->de", inputs, d_keyval, preferred_element_type=jnp.float32
        )
        d_inputs = jnp.einsum(
            "rle,de->rld", d_keyval, w_mix[:, D:], preferred_element_type=jnp.float32
        )
        d_picked = d_sum + jnp.einsum(
            "rse,de->rsd", d_query, w_mix[:, :D], preferred_element_type=jnp.float32
        )
        d_inputs = (
            d_inputs.reshape(per_step, SLOTS, QLEN, D)
            .at[:, :, 0]
            .add(d_picked)
            .reshape(per_step, SEQ_LEN, D)
        )
        grad_parts.append(d_inputs)
        step_terms = (
            jnp.concatenate([step_query, step_keyval], axis=1)[None],
            step_proj[None],
            step_up[None],
            step_down[None],
            d_gain_one[None],
            d_shift_one[None],
            d_gain_two[None],
            d_shift_two[None],
        )
        if totals is None:
            totals = tuple(step_terms)
        else:
            totals = tuple((left + right for left, right in zip(totals, step_terms)))
    shards = (
        lax.psum_scatter(totals[0], "batch", scatter_dimension=1, tiled=True),
        lax.psum_scatter(totals[1], "batch", scatter_dimension=1, tiled=True),
        lax.psum_scatter(totals[2], "batch", scatter_dimension=1, tiled=True),
        lax.psum_scatter(totals[3], "batch", scatter_dimension=1, tiled=True),
        lax.psum_scatter(totals[4], "batch", scatter_dimension=1, tiled=True),
        lax.psum_scatter(totals[5], "batch", scatter_dimension=1, tiled=True),
        lax.psum_scatter(totals[6], "batch", scatter_dimension=1, tiled=True),
        lax.psum_scatter(totals[7], "batch", scatter_dimension=1, tiled=True),
    )
    states_grad = jnp.concatenate(grad_parts)[None]
    return (
        loss_value,
        encoded,
        states_grad,
        shards[0],
        shards[1],
        shards[2],
        shards[3],
        shards[4],
        shards[5],
        shards[6],
        shards[7],
    )


def solution(mesh):
    placed = (
        P("tower", "batch", None, None),
        P("batch", None),
        P(),
        P("batch"),
        P("tower", "batch", None),
        P("tower", "batch", None),
        P("tower", "batch", None),
        P("tower", "batch", None),
        P("tower", "batch"),
        P("tower", "batch"),
        P("tower", "batch"),
        P("tower", "batch"),
    )
    return jax.shard_map(
        body,
        mesh=mesh,
        in_specs=placed,
        out_specs=(
            P(),
            P("tower", "batch", None, None),
            P("tower", "batch", None, None),
            P("tower", "batch", None),
            P("tower", "batch", None),
            P("tower", "batch", None),
            P("tower", "batch", None),
            P("tower", "batch"),
            P("tower", "batch"),
            P("tower", "batch"),
            P("tower", "batch"),
        ),
        check_vma=False,
    )
```

profile of v0, /device:TPU:0, one launch (start us, length us, event | category | flops | bytes accessed | tf_op | source)
XLA Modules:
  0.0 1820.7 jit_solution(13708447391511341190)
XLA Ops:
  15.6 44.3 %all-reduce.9 = (bf16[768]{0:T(1024)(128)(2,1)S(1)}, bf16[768]{0:T(1024)(128)(2,1)S(1)}, bf16[768]{0:T(1024)(128)(2,1)S(1)}, bf16[768]{0:T(1024)(128)(2,1)S(1)}) all-reduce(bf16[768]{0:T(1024)(128)(2,1)S(1)} %dynamic-update-slice.10, bf16[768]{0:T(1024)(128)(2,1)S(1)} %dynamic-update-slice.9, ...), channel_id=1, replica_groups=mesh['tower'=2,'batch'=16] {'batch'}, use_global_device_ids=true, to_apply=%add.3 | all-reduce | flops 3072 | bytes 12288
  68.3 17.3 all-gather.6.cloned.1.call-done
  175.3 6.6 fusion.530
  188.7 6.9 fusion.536
  202.2 7.0 fusion.533
  216.9 8.3 all-gather.10.cloned.1.call-done
  225.2 11.0 fusion.189
  236.3 70.7 %all-gather.12.cloned.1.call-done = bf16[1,3072,768]{2,1,0:T(8,128)(2,1)} async-done(((bf16[1,192,768]{2,1,0:T(8,128)(2,1)}), bf16[1,3072,768]{2,1,0:T(8,128)(2,1)}) %all-gather.12.cloned.1.call-update) | async-done | bytes 4718608 | tf_op jit(solution)/shard_map/all_gather | solution.py:113
  307.0 19.8 %fusion.535 = (f32[2,256]{1,0:T(2,128)S(1)}, f32[2,256,768]{2,1,0:T(8,128)S(1)}) fusion(bf16[1,3072,768]{2,1,0:T(8,128)(2,1)} %all-gather.12.cloned.1.call-done, f32[2,256,3072]{2,1,0:T(8,128)} %get-tuple-element.211, u8[256,3072]{1,0:T(8,128)(4,1)} %get-tuple-element.105, u8[256,3072]{1,0:T(8,128)(4,1)S(1)} %get-tuple-element.104, ...), kind=kOutput, calls=%fused_computation.749 | convolution fusion | flops 2528378368 | bytes 15740928 | tf_op jit(solution)/shard_map/rlf,fd->rld/dot_general | solution.py:83
  331.3 16.9 fusion.538
  352.8 16.9 fusion.532
  373.2 69.3 %all-gather = bf16[192,1,768]{2,1,0:T(2,128)(2,1)S(1)} all-gather(bf16[6,1,768]{2,1,0:T(2,128)(2,1)S(1)} %slice.267), channel_id=2, replica_groups=mesh['tower'=2,'batch'=16] {'tower','batch'}, dimensions={0}, use_global_device_ids=true | all-gather | bytes 304128 | tf_op jit(solution)/shard_map/all_gather | solution.py:129
  444.6 70.9 %fusion = f32[8,768]{1,0:T(8,128)S(1)} fusion(f32[192,768]{1,0:T(8,128)S(1)} %concatenate.74), kind=kCustom, calls=%all-reduce-scatter | all-reduce-scatter fusion | flops 196609 | bytes 614400
  522.1 5.5 collective-permute-start.3
  627.9 16.8 copy.343
  652.4 5.5 fusion.7
  669.6 46.3 %psum.7 = f32[]{:T(128)} all-reduce(f32[]{:T(128)S(6)} %div.235), channel_id=1, replica_groups=mesh['tower'=2,'batch'=16] {'tower','batch'}, use_global_device_ids=true, to_apply=%region_24.25 | all-reduce | flops 1 | bytes 8 | tf_op jit(solution)/shard_map/psum | solution.py:150
  744.9 100.1 %reduce-scatter.24.cloned.1.call-done = f32[48,1]{1,0:T(8,128)} async-done(((f32[768,1]{1,0:T(8,128)}), f32[48,1]{1,0:T(8,128)}) %reduce-scatter.24.cloned.1.call-update) | async-done | bytes 208
  846.3 124.0 %reduce-scatter.28.cloned.1.call-done = f32[48,1]{1,0:T(8,128)} async-done(((f32[768,1]{1,0:T(8,128)}), f32[48,1]{1,0:T(8,128)}) %reduce-scatter.28.cloned.1.call-update) | async-done | bytes 208
  971.7 124.8 %reduce-scatter.30.cloned.1.call-done = f32[48,1]{1,0:T(8,128)} async-done(((f32[768,1]{1,0:T(8,128)}), f32[48,1]{1,0:T(8,128)}) %reduce-scatter.30.cloned.1.call-update) | async-done | bytes 208
  1097.8 230.8 %all-reduce.12.cloned.1.call-done = f32[1,768,2304]{2,0,1:T(1,128)} async-done(((f32[1,768,2304]{2,0,1:T(1,128)}), f32[1,768,2304]{2,0,1:T(1,128)}) %all-reduce.12.cloned.1.call-update) | async-done | bytes 7077904
  1330.4 130.2 %reduce-scatter.18.cloned.1.call-done = f32[1,48,768]{2,1,0:T(8,128)} async-done(((f32[1,768,768]{2,1,0:T(8,128)}), f32[1,48,768]{2,1,0:T(8,128)}) %reduce-scatter.18.cloned.1.call-update) | async-done | bytes 147472 | tf_op jit(solution)/shard_map/reduce_scatter | solution.py:287
  1460.6 176.6 %reduce-scatter.22.cloned.1.call-done = f32[1,192,768]{2,1,0:T(8,128)} async-done(((f32[1,3072,768]{2,1,0:T(8,128)}), f32[1,192,768]{2,1,0:T(8,128)}) %reduce-scatter.22.cloned.1.call-update) | async-done | bytes 589840 | tf_op jit(solution)/shard_map/reduce_scatter | solution.py:289
  1637.1 176.3 %reduce-scatter.20.cloned.1.call-done = f32[1,48,3072]{2,1,0:T(8,128)} async-done(((f32[1,768,3072]{2,1,0:T(8,128)}), f32[1,48,3072]{2,1,0:T(8,128)}) %reduce-scatter.20.cloned.1.call-update) | async-done | bytes 589840 | tf_op jit(solution)/shard_map/reduce_scatter | solution.py:288
  (671 shorter events, 298.6 us)
Async XLA Ops:
  7.2 78.3 %all-gather.6.cloned.1.call-start = ((), (), s32[]{:S(2)}) async-start(), calls=%async_computation.7 | async-start | bytes 3760128 | tf_op jit(solution)/shard_map/all_gather | solution.py:110
  7.9 156.5 %all-gather.8.cloned.1.call-start = ((), (), s32[]{:S(2)}) async-start(), calls=%async_computation.8 | async-start | bytes 1253376 | tf_op jit(solution)/shard_map/all_gather | solution.py:111
  8.7 216.5 %all-gather.10.cloned.1.call-start = ((), (), s32[]{:S(2)}) async-start(), calls=%async_computation.9 | async-start | bytes 5013504 | tf_op jit(solution)/shard_map/all_gather | solution.py:112
  9.4 297.6 %all-gather.12.cloned.1.call-start = ((), (), s32[]{:S(2)}) async-start(), calls=%async_computation.10 | async-start | bytes 5013504 | tf_op jit(solution)/shard_map/all_gather | solution.py:113
  10.0 733.6 %reduce-scatter.26.cloned.1.call-start = ((), (), s32[]{:S(2)}) async-start(), calls=%async_computation.15 | async-start | bytes 417792
  225.2 101.6 %slice-start = ((s8[4718592]{0:T(1024)(128)(4,1)}), s8[524288]{0:T(1024)(128)(4,1)S(1)}, s32[]{:S(2)}) async-start(s8[4718592]{0:T(1024)(128)(4,1)} %bitcast.458), calls=%async_computation.19 | async-start | bytes 1048576
  370.7 156.8 %copy-start.30 = (f32[2,4,768]{2,1,0:T(4,128)S(1)}, f32[2,4,768]{2,1,0:T(4,128)}, u32[]{:S(2)}) copy-start(f32[2,4,768]{2,1,0:T(4,128)} %copy-done.29) | copy-start | bytes 73732
  370.7 156.8 %copy-start.104 = (f32[2,4]{1,0:T(2,128)S(1)}, f32[2,4]{1,0:T(2,128)}, u32[]{:S(2)}) copy-start(f32[2,4]{1,0:T(2,128)} %copy-done.103) | copy-start | bytes 100
  370.8 156.8 %copy-start.115 = (f32[2,4]{1,0:T(2,128)S(1)}, f32[2,4]{1,0:T(2,128)}, u32[]{:S(2)}) copy-start(f32[2,4]{1,0:T(2,128)} %fusion.390) | copy-start | bytes 100
  515.5 29.7 %collective-permute-start.6 = (f32[8,768]{1,0:T(8,128)S(1)}, f32[8,768]{1,0:T(8,128)S(1)}, u32[]{:S(2)}, u32[]{:S(2)}) collective-permute-start(f32[8,768]{1,0:T(8,128)S(1)} %fusion), channel_id=1, source_target_pairs={{0,7},{1,8},{2,9},{3,10},{4,11},{5,12},{6,13},{7,14},{8,15},{9,16}... | collective-permute-start | bytes 73736
  516.8 32.2 %collective-permute-start.5 = (f32[8,768]{1,0:T(8,128)S(1)}, f32[8,768]{1,0:T(8,128)S(1)}, u32[]{:S(2)}, u32[]{:S(2)}) collective-permute-start(f32[8,768]{1,0:T(8,128)S(1)} %fusion), channel_id=1, source_target_pairs={{0,6},{1,7},{2,8},{3,9},{4,10},{5,11},{6,12},{7,13},{8,14},{9,15},... | collective-permute-start | bytes 73736
  519.2 31.5 %collective-permute-start.4 = (f32[8,768]{1,0:T(8,128)S(1)}, f32[8,768]{1,0:T(8,128)S(1)}, u32[]{:S(2)}, u32[]{:S(2)}) collective-permute-start(f32[8,768]{1,0:T(8,128)S(1)} %fusion), channel_id=1, source_target_pairs={{0,5},{1,6},{2,7},{3,8},{4,9},{5,10},{6,11},{7,12},{8,13},{9,14},{... | collective-permute-start | bytes 73736
  522.1 28.6 %collective-permute-start.3 = (f32[8,768]{1,0:T(8,128)S(1)}, f32[8,768]{1,0:T(8,128)S(1)}, u32[]{:S(2)}, u32[]{:S(2)}) collective-permute-start(f32[8,768]{1,0:T(8,128)S(1)} %fusion), channel_id=1, source_target_pairs={{0,4},{1,5},{2,6},{3,7},{4,8},{5,9},{6,10},{7,11},{8,12},{9,13},{1... | collective-permute-start | bytes 73736
  539.0 2.8 collective-permute-start.7
  541.8 8.9 collective-permute-start.2
  545.3 5.4 collective-permute-start.1
  549.1 3.1 collective-permute-start
  593.0 252.0 %reduce-scatter.24.cloned.1.call-start = ((), (), s32[]{:S(2)}) async-start(), calls=%async_computation.14 | async-start | bytes 417792
  599.3 371.0 %reduce-scatter.28.cloned.1.call-start = ((), (), s32[]{:S(2)}) async-start(), calls=%async_computation.16 | async-start | bytes 417792
  601.1 495.4 %reduce-scatter.30.cloned.1.call-start = ((), (), s32[]{:S(2)}) async-start(), calls=%async_computation.17 | async-start | bytes 417792
  614.2 714.3 %all-reduce.12.cloned.1.call-start = ((), (), s32[]{:S(2)}) async-start(), calls=%async_computation.18 | async-start | bytes 14155776
  644.7 815.9 %reduce-scatter.18.cloned.1.call-start = ((), (), s32[]{:S(2)}) async-start(), calls=%async_computation.11 | async-start | bytes 2506752 | tf_op jit(solution)/shard_map/reduce_scatter | solution.py:287
  648.5 988.6 %reduce-scatter.22.cloned.1.call-start = ((), (), s32[]{:S(2)}) async-start(), calls=%async_computation.13 | async-start | bytes 10027008 | tf_op jit(solution)/shard_map/reduce_scatter | solution.py:289
  658.0 1155.4 %reduce-scatter.20.cloned.1.call-start = ((), (), s32[]{:S(2)}) async-start(), calls=%async_computation.12 | async-start | bytes 10027008 | tf_op jit(solution)/shard_map/reduce_scatter | solution.py:288
  (181 other events, 1987.3 us)
Sparse Core Ops, SparseCore 0:
  10.8 74.6 all-gather.5
  88.3 54.6 all-gather.7
  145.8 79.3 all-gather.9
  227.9 79.0 all-gather.11
  593.2 125.5 reduce-scatter.25
  724.6 120.3 reduce-scatter.23
  849.7 120.6 reduce-scatter.27
  975.7 120.7 reduce-scatter.29
  1102.7 225.7 all-reduce.11
  1333.9 126.6 reduce-scatter.17
  1467.8 169.3 reduce-scatter.21
  1643.2 170.1 reduce-scatter.19
where the time goes:
time: 1830 us; the launch traced here: 1820 us
  waiting for transfers between devices  1160 us (63%)
  blocking collectives  231 us (13%)
  matrix products  231 us (13%)
  local copies, waits for them, and re-layouts  122 us (7%)
  other arithmetic  30.9 us (2%)
  starting transfers between devices  23 us (1%)
  between operations  19.5 us (1%)
    unnamed x25, waiting for transfers between devices  585 us
    reduce_scatter x1, waiting for transfers between devices, body(): lax.psum_scatter(totals[3], 'batch', scatter_dimension=1, tiled=True)  177 us
    reduce_scatter x1, waiting for transfers between devices, body(): lax.psum_scatter(totals[2], 'batch', scatter_dimension=1, tiled=True)  176 us
    reduce_scatter x1, waiting for transfers between devices, body(): lax.psum_scatter(totals[1], 'batch', scatter_dimension=1, tiled=True)  130 us
    unnamed x2, blocking collectives  115 us
    all_gather x1, waiting for transfers between devices, body(): lax.all_gather(w_back, 'batch', axis=1, tiled=True)  70.7 us
    all_gather x1, blocking collectives, body(): everyone = lax.all_gather(own_heads, ('tower', 'batch'), axis=0, tiled=True)  69.3 us
    dot_general x3, matrix products, encode(): jnp.einsum('rlf,fd->rld', active, w_down, preferred_element_type=jnp.floa...  53.7 us
  transfers between devices with their start and end apart: 20, of which 12 were waited for; matrix products, arithmetic and copies ran while one was open for 15% of the time, Pallas kernels for 0%

commit v1 on v0

v1 whole, which is shorter than its diff:
```python
import functools
import math

import jax
import jax.numpy as jnp
from jax import lax
from jax.experimental import pallas as pl
from jax.experimental.pallas import tpu as pltpu
from jax.sharding import PartitionSpec as P

D = 768
HEADS = 12
HEAD = 64
FF = 3072
SEQ_LEN = 256
QLEN = 64
SLOTS = 4
EPS = 1e-05
NEG = -1000000000.0
BF = jnp.bfloat16
F32 = jnp.float32
MIB = 1 << 20
HEAD_SCALE = 1.0 / math.sqrt(HEAD)
LOGIT_SCALE = 2.0 / math.sqrt(D)
CHUNKS = FF // D
VMEM = pl.BlockSpec(memory_space=pltpu.VMEM)
SMEM = pl.BlockSpec(memory_space=pltpu.SMEM)
ANY = pl.BlockSpec(memory_space=pl.ANY)


def dot(a, b):
    return lax.dot_general(a, b, (((1,), (0,)), ((), ())), preferred_element_type=F32)


def dot_nt(a, b):
    return lax.dot_general(a, b, (((1,), (1,)), ((), ())), preferred_element_type=F32)


def dot_tn(a, b):
    return lax.dot_general(a, b, (((0,), (0,)), ((), ())), preferred_element_type=F32)


def iota(shape, axis):
    return lax.broadcasted_iota(jnp.int32, shape, axis)


def normalise(summed):
    center = summed - jnp.mean(summed, axis=-1, keepdims=True)
    spread = jnp.mean(center * center, axis=-1, keepdims=True)
    scale = lax.rsqrt(spread + EPS)
    return center * scale, scale


def normalise_back(grad, hat, scale, gain):
    d_hat = grad * gain
    mean_d = jnp.mean(d_hat, axis=-1, keepdims=True)
    mean_dh = jnp.mean(d_hat * hat, axis=-1, keepdims=True)
    d_gain = jnp.sum(grad * hat, axis=0, keepdims=True)
    d_shift = jnp.sum(grad, axis=0, keepdims=True)
    return scale * (d_hat - mean_d - hat * mean_dh), d_gain, d_shift


def normal_cdf(values):
    return 0.5 * (1.0 + lax.erf(values * math.sqrt(0.5)))


def gelu(values):
    return values * normal_cdf(values)


def gelu_pair(values):
    cdf = normal_cdf(values)
    bell = jnp.exp(-0.5 * values * values) * (1.0 / math.sqrt(2.0 * math.pi))
    return values * cdf, cdf + values * bell


class Links:
    def __init__(self):
        def table(move):
            at = lambda z, y, x: z * 4 + y * 2 + x
            return [
                (at(z, y, x), at(*move(z, y, x)))
                for z in range(4)
                for y in range(2)
                for x in range(2)
            ]

        self.x = table(lambda z, y, x: (z, y, 1 - x))
        self.y = table(lambda z, y, x: (z, 1 - y, x))
        self.z = [table(lambda z, y, x, c=c: ((z + c) % 4, y, x)) for c in range(4)]
        me = lax.axis_index("batch")
        self.at = (me // 4, me // 2 % 2, me % 2)


def move(value, pairs):
    return lax.ppermute(value, "batch", pairs)


def after(value, *earlier):
    late = sum(other[(0,) * other.ndim].astype(F32) for other in earlier) > 1e30
    return jnp.where(late, jnp.zeros_like(value), value)


ORDER = (0, 1, 3, 2)


def gather_line(links, shard):
    return [shard] + [move(shard, links.z[c]) for c in ORDER[1:]]


def gather_plane(links, line):
    near = [(block, move(block, links.x), move(block, links.y)) for block in line]
    pieces = []
    for k, (block, by_x, by_y) in enumerate(near):
        far = move(by_x, links.y) if k % 2 == 0 else move(by_y, links.x)
        pieces += [block, by_x, by_y, far]
    return pieces


def piece_places(links):
    z, y, x = links.at
    place = lambda c, dy, dx: (z - c + 4) % 4 * 4 + (y ^ dy) * 2 + (x ^ dx)
    order = [(c, dy, dx) for c in ORDER for dy in range(2) for dx in range(2)]
    return jnp.stack([place(*at) for at in order]).astype(jnp.int32)


class Gathered:
    def __init__(self, pieces, place):
        self.pieces = [piece[None] for piece in pieces]
        self.place = place
        self.blocks = place.shape[0]

    def whole(self):
        return self.pieces[0][0]


def gather_whole(shard):
    whole = lax.all_gather(shard, "batch", axis=0, tiled=True)
    return Gathered([whole], jnp.zeros((1,), jnp.int32))


def gather_rows(links, rows, cut):
    if links is None:
        full = lax.all_gather(rows, "batch", axis=0, tiled=True)
        return full[:, :cut], full[:, cut:]
    z, y, x = links.at
    count, width = rows.shape
    zs = [rows] + [move(rows, links.z[c]) for c in (1, 2, 3)]
    line = jnp.concatenate([zs[3], zs[2], zs[1], zs[0], zs[3], zs[2], zs[1]])
    line = lax.dynamic_slice(line, ((3 - z) * count, 0), (4 * count, width))
    left, right = line[:, :cut], line[:, cut:]

    def both(part, pairs, at):
        other = move(part, pairs)
        return jnp.where(at == 0, jnp.stack([part, other]), jnp.stack([other, part]))

    left = both(both(left, links.x, x), links.y, y)
    right = both(both(right, links.y, y), links.x, x)
    left = left.reshape(2, 2, 4, count, cut).transpose(2, 0, 1, 3, 4)
    right = right.reshape(2, 2, 4, count, width - cut).transpose(2, 1, 0, 3, 4)
    return left.reshape(16 * count, cut), right.reshape(16 * count, width - cut)


def low_sum(a, b):
    return (a.astype(F32) + b.astype(F32)).astype(BF)


def load(group, target, sems, low=0):
    place, pieces = group
    copies = []
    for piece in pieces:
        for c in range(piece.shape[0]):
            k = len(copies)
            unit = piece.shape[1]
            row = pl.multiple_of(place[k] * unit, unit)
            copies.append(
                pltpu.make_async_copy(
                    piece.at[c, :, pl.ds(low, target.shape[1])],
                    target.at[pl.ds(row, unit), :],
                    sems.at[k],
                )
            )
    for copy in copies:
        copy.start()
    return copies


def wait_all(copies):
    for copy in copies:
        copy.wait()


def launch(
    kernel, ins, weights, outs, scratch, room, grid=None, flops=0, moved=0, same=None, behind=()
):
    values = list(ins)
    for weight in weights:
        values += [(weight.place, SMEM)] + [(piece, ANY) for piece in weight.pieces]
    values += [(value, ANY) for value in behind]

    def run(*refs):
        at = len(ins)
        groups = []
        for weight in weights:
            end = at + 1 + len(weight.pieces)
            groups.append((refs[at], refs[at + 1 : end]))
            at = end
        at += len(behind)
        kernel(refs[: len(ins)], groups, refs[at : at + len(outs)], refs[at + len(outs) :])

    extra = {} if grid is None else {"grid": grid}
    return pl.pallas_call(
        run,
        name=getattr(kernel, "func", kernel).__name__,
        input_output_aliases=same or {},
        in_specs=[spec for _, spec in values],
        out_specs=[spec for _, _, spec in outs],
        out_shape=[jax.ShapeDtypeStruct(shape, dtype) for shape, dtype, _ in outs],
        scratch_shapes=scratch,
        compiler_params=pltpu.CompilerParams(vmem_limit_bytes=room * MIB),
        cost_estimate=pl.CostEstimate(
            flops=int(flops), bytes_accessed=int(moved), transcendentals=0
        ),
        **extra,
    )(*[value for value, _ in values])


def sems(*shape):
    return pltpu.SemaphoreType.DMA(shape)


def rows_spec(many, *tail, skip=0):
    return pl.BlockSpec((many,) + tail, lambda r: (r + skip,) + (0,) * len(tail))


def open_keys(shape, key_axis, row, slot_of_query, lens, ask):
    key_at = iota(shape, key_axis)
    slot = key_at >> 6
    limit = jnp.zeros(shape, jnp.int32)
    for s in range(SLOTS):
        limit = jnp.where(slot == s, lens[row, s] * ask + QLEN * (1 - ask), limit)
    return ((key_at & (QLEN - 1)) < limit) & (slot_of_query * ask == slot * ask)


def mix(skip, ins, groups, outs, scratch):
    lens, asking, x_ref = ins[:3]
    query_ref, key_ref, value_ref, context_ref = outs[:4]
    w, w_gain, w_turned, sem = scratch
    row = pl.program_id(0) + skip

    @pl.when(pl.program_id(0) == 0)
    def _():
        copies = load(groups[0], w, sem.at[0])
        if len(outs) > 4:
            wait_all(load(groups[0], w_gain, sem.at[1], 4 * D))
            outs[4][...] = w_gain[...].astype(F32).T[:8]
        wait_all(copies)
        for j in range(0, D, 128):
            part = w[:, 2 * D + j : 2 * D + j + 128].astype(F32)
            w_turned[j : j + 128, :] = part.T.astype(BF)

    x = x_ref[0]
    mixed = dot(x, w[:, : 2 * D])
    for s in range(SLOTS):
        query_ref[0, s : s + 1, :] = mixed[s * QLEN : s * QLEN + 1, :D]
    query = (mixed[:, :D] * HEAD_SCALE).astype(BF)
    keyset = mixed[:, D:].astype(BF)
    values = dot_nt(w_turned[...], x).astype(BF)
    key_ref[0] = keyset
    value_ref[0] = values
    shape = (SEQ_LEN, SEQ_LEN)
    closed = jnp.where(open_keys(shape, 0, row, iota(shape, 1) >> 6, lens, asking[0]), 0, 1) == 1
    ones = jnp.ones((16, SEQ_LEN), BF)
    nothing = jnp.zeros((SEQ_LEN, 128), BF)
    half_of = iota((SEQ_LEN, 128), 1) // HEAD
    scores = []
    for head in range(HEADS):
        low = head // 2 * 128
        mine = jnp.where(half_of == head % 2, query[:, low : low + 128], nothing)
        scores.append(dot_nt(keyset[:, low : low + 128], mine))
    expos = []
    for score in scores:
        score = jnp.where(closed, NEG, score)
        expos.append(jnp.exp(score - jnp.max(score, axis=0, keepdims=True)).astype(BF))
    parts = []
    for head, expo in enumerate(expos):
        mine = values[head * HEAD : head * HEAD + HEAD]
        summed = dot(jnp.concatenate([mine, ones], axis=0), expo)
        parts.append(summed[:HEAD] / summed[HEAD : HEAD + 1])
    context_ref[0] = jnp.concatenate(parts, axis=0).T.astype(BF)


def up(ins, groups, outs, scratch):
    x_ref, context_ref, gains = ins
    first_ref, act_ref = outs
    w_out, w_in, sem = scratch

    @pl.when(pl.program_id(0) == 0)
    def _():
        wait_all(load(groups[0], w_out, sem.at[0], 3 * D) + load(groups[1], w_in, sem.at[1]))

    many = x_ref.shape[0] * SEQ_LEN
    attended = dot(context_ref[...].reshape(many, D), w_out[...])
    summed = x_ref[...].reshape(many, D).astype(F32) + attended
    first = normalise(summed)[0] * gains[0:1] + gains[1:2]
    low = first.astype(BF)
    first_ref[...] = low.reshape(first_ref.shape)
    for j in range(CHUNKS):
        part = gelu(dot(low, w_in[:, j * D : j * D + D])).astype(BF)
        act_ref[:, :, j * D : j * D + D] = part.reshape(act_ref.shape[0], SEQ_LEN, D)


def down(ins, groups, outs, scratch):
    first_ref, act_ref, gains = ins
    (encoded_ref,) = outs
    w_back, sem = scratch

    @pl.when(pl.program_id(0) == 0)
    def _():
        wait_all(load(groups[0], w_back, sem))

    many = first_ref.shape[0] * SEQ_LEN
    summed = dot(act_ref[...].reshape(many, FF), w_back[...])
    hat = normalise(first_ref[...].reshape(many, D).astype(F32) + summed)[0]
    encoded_ref[...] = (hat * gains[2:3] + gains[3:4]).astype(BF).reshape(encoded_ref.shape)


def head_up_math(context, picked, gains, w_out, w_in, emit):
    hat, scale = normalise(picked.astype(F32) + dot(context, w_out))
    low = (hat * gains[0:1] + gains[1:2]).astype(BF)
    for j in range(CHUNKS):
        act, slope = gelu_pair(dot(low, w_in(j)))
        emit(j, act.astype(BF), slope.astype(BF))
    return hat, scale, low


def head_up(ins, groups, outs, scratch):
    context_ref, picked_ref, gains = ins
    hat_ref, scale_ref, low_ref, act_ref, slope_ref = outs
    w_out, w_in, sem = scratch
    wait_all(load(groups[0], w_out, sem.at[0], 3 * D) + load(groups[1], w_in, sem.at[1]))

    def emit(j, act, slope):
        act_ref[:, j * D : j * D + D] = act
        slope_ref[:, j * D : j * D + D] = slope

    hat, scale, low = head_up_math(
        context_ref[...],
        picked_ref[...],
        gains[...],
        w_out[...],
        lambda j: w_in[:, j * D : j * D + D],
        emit,
    )
    hat_ref[...] = hat
    scale_ref[...] = jnp.broadcast_to(scale, scale_ref.shape)
    low_ref[...] = low


def head_down_math(hat, gains, act, w_back):
    hat2, scale2 = normalise(hat * gains[0:1] + gains[1:2] + dot(act, w_back))
    return hat2, scale2, (hat2 * gains[2:3] + gains[3:4]).astype(BF)


def head_down(ins, groups, outs, scratch):
    hat_ref, act_ref, gains = ins
    hat2_ref, scale2_ref, final_ref = outs
    w_back, sem = scratch
    wait_all(load(groups[0], w_back, sem))
    hat2, scale2, final = head_down_math(hat_ref[...], gains[...], act_ref[...], w_back[...])
    hat2_ref[...] = hat2
    scale2_ref[...] = jnp.broadcast_to(scale2, scale2_ref.shape)
    final_ref[...] = final


def logit_back(asked, passages, positives, ids, place_of):
    logits = dot_nt(asked, passages) * LOGIT_SCALE
    chosen = positives == place_of
    asked_data = jnp.sum(jnp.where(chosen, ids, 0.0), axis=1, keepdims=True)
    open_to = (asked_data == ids) & (place_of >= 0)
    masked = jnp.where(open_to, logits, NEG)
    highest = jnp.max(masked, axis=1, keepdims=True)
    expo = jnp.exp(masked - highest)
    total = jnp.sum(expo, axis=1, keepdims=True)
    target = jnp.sum(jnp.where(chosen, logits, 0.0), axis=1, keepdims=True)
    loss = jnp.sum(highest + jnp.log(total) - target, axis=0, keepdims=True) / asked.shape[0]
    d_logits = (expo / total - jnp.where(chosen, 1.0, 0.0)) * (LOGIT_SCALE / asked.shape[0])
    return loss, d_logits


def dot_split(a, b):
    high = a.astype(BF)
    return dot(high, b) + dot((a - high.astype(F32)).astype(BF), b)


def back_math(d_final, hat2, scale2, hat, scale, gains, slope, w_out, w_in, w_back, emit):
    d_second, d_gain2, d_shift2 = normalise_back(d_final, hat2, scale2, gains[2:3])
    d_down = d_second.astype(BF)
    d_first = d_second
    for j in range(CHUNKS):
        d_up = (dot_nt(d_down, w_back(j)) * slope(j).astype(F32)).astype(BF)
        emit(j, d_up)
        d_first = d_first + dot_nt(d_up, w_in(j))
    d_sum, d_gain, d_shift = normalise_back(d_first, hat, scale, gains[0:1])
    d_att = d_sum.astype(BF)
    d_context = None if w_out is None else dot_nt(d_att, w_out())
    return d_down, d_sum, d_att, d_context, (d_gain, d_shift, d_gain2, d_shift2)


def head_back(ins, groups, outs, scratch):
    asking, own, mine_ref, other_ref, positives, ids, place_of, gains = ins[:8]
    hat2_ref, scale2_ref, hat_ref, scale_ref, slope_ref = ins[8:13]
    act_part, low_part, context_part = ins[13:]
    loss_ref, context_ref, sum_ref, gain_ref, grad_out, grad_in, grad_back = outs
    w_out, w_in, w_back, d_ups, keep_sum, keep_context, sem = scratch
    from_back = load(groups[2], w_back, sem.at[0])
    from_in = load(groups[1], w_in, sem.at[1])
    from_out = load(groups[0], w_out, sem.at[2], 3 * D)
    rows = mine_ref.shape[0]
    is_asking = jnp.full((rows, D), asking[0]) == 1
    mine, other = mine_ref[...], other_ref[...]
    loss, d_logits = logit_back(
        jnp.where(is_asking, mine, other),
        jnp.where(is_asking, other, mine),
        positives[...],
        ids[...],
        place_of[...],
    )
    loss_ref[...] = jnp.broadcast_to(loss, loss_ref.shape)
    square = jnp.full((rows, rows), asking[0]) == 1
    d_final = dot_split(jnp.where(square, d_logits, d_logits.T), other)
    wait_all(from_back)
    wait_all(from_in + from_out)

    def emit(j, d_up):
        d_ups[:, j * D : j * D + D] = d_up

    d_down, d_sum, d_att, d_context, d_gains = back_math(
        d_final,
        hat2_ref[...],
        scale2_ref[:, :1],
        hat_ref[...],
        scale_ref[:, :1],
        gains[...],
        lambda j: slope_ref[:, j * D : j * D + D],
        lambda: w_out[...],
        lambda j: w_in[:, j * D : j * D + D],
        lambda j: w_back[j * D : j * D + D, :],
        emit,
    )
    for i, d_gain in enumerate(d_gains):
        gain_ref[i : i + 1, :] = d_gain
    keep_sum[...] = d_sum
    keep_context[...] = d_context
    count = sum_ref.shape[0] * SLOTS
    at = pl.ds(pl.multiple_of(own[0] * count, 8), count)
    own_sum, own_context = keep_sum[at, :], keep_context[at, :]
    for r in range(sum_ref.shape[0]):
        sum_ref[r] = own_sum[r * SLOTS : r * SLOTS + SLOTS]
        context_ref[r] = own_context[r * SLOTS : r * SLOTS + SLOTS]
    grad_back[...] = dot_tn(act_part[...], d_down)
    grad_in[...] = dot_tn(low_part[...], d_ups[...])
    grad_out[...] = dot_tn(context_part[...], d_att)


WIDE = HEADS * SLOTS


def spread_heads(four):
    eight = jnp.concatenate([four, four], axis=0)
    tall = jnp.concatenate([eight] * (HEADS // 2), axis=0)
    return jnp.where(own_head(), tall, 0.0)


def own_head():
    shape = (WIDE, D)
    return iota(shape, 0) // SLOTS == iota(shape, 1) // HEAD


def attend_back(ins, groups, outs, scratch):
    source, lens, asking, x_ref, picked_ref, key_ref, value_ref, context_ref = ins
    probs_ref, score_ref, query_ref, wide_ref, d_query_ref = outs[:5]
    sum_refs = outs[5:]
    seen, full, total = scratch
    step = pl.program_id(0)
    many = x_ref.shape[0]
    shape = (WIDE, SEQ_LEN)
    every = range(many)
    slot_of = iota(shape, 0) & (SLOTS - 1)
    valid = [open_keys(shape, 1, step * many + i, slot_of, lens, asking[0]) for i in every]
    query = [spread_heads(picked_ref[i]).astype(BF) for i in every]
    d_context = [spread_heads(context_ref[i]).astype(BF) for i in every]
    score = [dot_nt(query[i], key_ref[i]) * HEAD_SCALE for i in every]
    d_probs = [dot(d_context[i], value_ref[i]) for i in every]
    probs, d_score = [], []
    for i in every:
        masked = jnp.where(valid[i], score[i], NEG)
        expo = jnp.exp(masked - jnp.max(masked, axis=-1, keepdims=True))
        prob = expo / jnp.sum(expo, axis=-1, keepdims=True)
        spread = jnp.sum(d_probs[i] * prob, axis=-1, keepdims=True)
        probs.append(prob.astype(BF))
        d_score.append((prob * (d_probs[i] - spread)).astype(BF))
    for i in every:
        probs_ref[i] = probs[i]
        score_ref[i] = d_score[i]
        query_ref[i] = query[i]
        wide_ref[i] = d_context[i]
    d_query = [dot(d_score[i], key_ref[i]) * HEAD_SCALE for i in every]
    by_key = [(dot(d_score[i], x_ref[i]) * HEAD_SCALE).astype(BF) for i in every]
    by_val = [dot(probs[i], x_ref[i]).astype(BF) for i in every]
    for i in every:
        kept = jnp.where(own_head(), d_query[i], 0.0)
        eight = kept[0:8]
        for j in range(8, WIDE, 8):
            eight = eight + kept[j : j + 8]
        d_query_ref[i] = (eight[:SLOTS] + eight[SLOTS:]).astype(BF)
        at = pl.ds(pl.multiple_of((step * many + i) * WIDE, 16), WIDE)
        seen[0, at, :] = by_key[i]
        seen[1, at, :] = by_val[i]
        full[0, at, :] = query[i]
        full[1, at, :] = d_context[i]

    @pl.when(step == pl.num_programs(0) - 1)
    def _():
        for which in range(2):
            total[...] = dot_tn(seen[which], full[which]).astype(BF)
            k = 0
            for out_ref in sum_refs[2 * which : 2 * which + 2]:
                blocks, unit = out_ref.shape[0], out_ref.shape[1]
                for i in range(blocks):
                    at = pl.multiple_of(source[which, k] * unit, unit)
                    out_ref[i] = total[pl.ds(at, unit), :]
                    k += 1


def states_back(ins, groups, outs, scratch):
    probs_ref, score_ref, query_ref, wide_ref, d_query_ref, d_sum_ref = ins
    (grad_ref,) = outs
    w, sem = scratch

    @pl.when(pl.program_id(0) == 0)
    def _():
        wait_all(load(groups[0], w, sem))

    many = grad_ref.shape[0]
    every = range(many)
    tall = many * WIDE
    by_key = (dot_nt(query_ref[...].reshape(tall, D), w[:, D : 2 * D]) * HEAD_SCALE).astype(BF)
    by_val = dot_nt(wide_ref[...].reshape(tall, D), w[:, 2 * D :]).astype(BF)
    fours = [d_query_ref[i].astype(F32) for i in every]
    extra = dot_nt(jnp.concatenate(fours, axis=0).astype(BF), w[:, :D])
    for i in every:
        rows = slice(i * WIDE, i * WIDE + WIDE)
        grad_ref[i] = dot_tn(score_ref[i], by_key[rows]) + dot_tn(probs_ref[i], by_val[rows])
        for s in range(SLOTS):
            at = slice(s * QLEN, s * QLEN + 1)
            add = extra[i * SLOTS + s : i * SLOTS + s + 1] + d_sum_ref[i, s : s + 1]
            grad_ref[i, at, :] = grad_ref[i, at, :] + add


def body(
    states,
    q_lengths,
    dataset_ids,
    positives,
    w_qkv,
    w_out,
    w_in,
    w_back,
    gain_first,
    bias_first,
    gain_second,
    bias_second,
):
    devices = lax.axis_size("batch")
    links = Links() if devices == 16 else None
    own = lax.axis_index("batch")
    is_asking = lax.axis_index("tower") == 0
    asking = is_asking.astype(jnp.int32).reshape(1)
    inputs = states[0]
    rows = inputs.shape[0]
    heads = rows * SLOTS
    every = heads * devices
    part = w_qkv.shape[1]
    back_part = w_back.shape[1]

    vectors = jnp.concatenate([gain_first, bias_first, gain_second, bias_second], axis=0)
    vectors = jnp.pad(vectors.T, ((0, 0), (0, 124)))
    first_needed = jnp.concatenate([w_qkv[0], w_out[0], vectors], axis=1)
    g_in = gather_whole(w_in[0])
    if links is not None:
        place = piece_places(links)
        mix_pieces = gather_plane(links, gather_line(links, first_needed))
        g_mix = Gathered(mix_pieces, place)
        back_line = gather_line(links, after(w_back[0], mix_pieces[12]))
        back_line[0] = after(w_back[0], mix_pieces[13], mix_pieces[14])
        back_pieces = gather_plane(links, back_line)
        g_back = Gathered(back_pieces, place)
    else:
        g_mix, g_back = gather_whole(first_needed), gather_whole(w_back[0])

    one = functools.partial(rows_spec, 1)
    two = functools.partial(rows_spec, 2)
    half = rows // 2
    mixed = []
    for skip in (0, half):
        at = functools.partial(rows_spec, 1, skip=skip)
        kept = [
            ((rows, SLOTS, D), F32, at(SLOTS, D)),
            ((rows, SEQ_LEN, D), BF, at(SEQ_LEN, D)),
            ((rows, D, SEQ_LEN), BF, at(D, SEQ_LEN)),
            ((rows, SEQ_LEN, D), BF, at(SEQ_LEN, D)),
        ]
        behind = []
        if links is not None:
            behind = [back_pieces[k] for k in ((1, 2, 5, 6, 9, 10) if skip else (4, 8, 12))]
        if skip:
            mixed, gains = mixed[:4], mixed[4]
        mixed = launch(
            functools.partial(mix, skip),
            [(q_lengths, SMEM), (asking, SMEM), (inputs, at(SEQ_LEN, D))]
            + [(value, ANY) for value in mixed],
            [g_mix],
            kept if skip else kept + [((8, D), F32, VMEM)],
            [
                pltpu.VMEM((D, 3 * D), BF),
                pltpu.VMEM((D, 128), BF),
                pltpu.VMEM((D, D), BF),
                sems(2, g_mix.blocks),
            ],
            room=60,
            grid=(half,),
            flops=2 * half * SEQ_LEN * D * (3 * D + 4 * SEQ_LEN),
            moved=10 * MIB,
            same={3 + k: k for k in range(4)} if skip else None,
            behind=behind,
        )
    query, key, value, context = mixed
    picked = inputs.reshape(rows, SLOTS, QLEN, D)[:, :, 0].reshape(heads, D)
    context_own = context.reshape(rows, SLOTS, QLEN, D)[:, :, 0].reshape(heads, D)
    index = positives[:, None]
    note = jnp.pad(jnp.concatenate([index // 256, index % 256], axis=1), ((0, 0), (0, 126)))
    parcel = jnp.concatenate([context_own, picked, note.astype(BF)], axis=1)
    context_all, shared = gather_rows(links, parcel, D)
    picked_all = shared[:, :D]
    noted = shared[:, D : D + 2].astype(jnp.int32)
    positives_all = noted[:, :1] * 256 + noted[:, 1:]

    if links is not None:
        first, act = launch(
            up,
            [(inputs, two(SEQ_LEN, D)), (context, two(SEQ_LEN, D)), (gains, VMEM)],
            [g_mix, g_in],
            [
                ((rows, SEQ_LEN, D), BF, two(SEQ_LEN, D)),
                ((rows, SEQ_LEN, FF), BF, two(SEQ_LEN, FF)),
            ],
            [pltpu.VMEM((D, D), BF), pltpu.VMEM((D, FF), BF), sems(2, g_mix.blocks)],
            room=40,
            grid=(rows // 2,),
            flops=2 * rows * SEQ_LEN * D * (D + FF),
            moved=30 * MIB,
        )

        hat, scale, low, head_act, slope = launch(
            head_up,
            [(context_all, VMEM), (picked_all, VMEM), (gains, VMEM)],
            [g_mix, g_in],
            [
                ((every, D), F32, VMEM),
                ((every, 128), F32, VMEM),
                ((every, D), BF, VMEM),
                ((every, FF), BF, VMEM),
                ((every, FF), BF, VMEM),
            ],
            [pltpu.VMEM((D, D), BF), pltpu.VMEM((D, FF), BF), sems(2, g_mix.blocks)],
            room=36,
            flops=2 * every * D * (D + FF),
            moved=14 * MIB,
            behind=[act],
        )
        hat2, scale2, final = launch(
            head_down,
            [(hat, VMEM), (head_act, VMEM), (gains, VMEM)],
            [g_back],
            [((every, D), F32, VMEM), ((every, 128), F32, VMEM), ((every, D), BF, VMEM)],
            [pltpu.VMEM((FF, D), BF), sems(g_back.blocks)],
            room=24,
            flops=2 * every * D * FF,
            moved=10 * MIB,
        )
    else:
        first, act = launch(
            up,
            [(inputs, two(SEQ_LEN, D)), (context, two(SEQ_LEN, D)), (gains, VMEM)],
            [g_mix, g_in],
            [
                ((rows, SEQ_LEN, D), BF, two(SEQ_LEN, D)),
                ((rows, SEQ_LEN, FF), BF, two(SEQ_LEN, FF)),
            ],
            [pltpu.VMEM((D, D), BF), pltpu.VMEM((D, FF), BF), sems(2, g_mix.blocks)],
            room=40,
            grid=(rows // 2,),
            flops=2 * rows * SEQ_LEN * D * (D + FF),
            moved=30 * MIB,
        )

        out_full = g_mix.whole()[:, 3 * D : 4 * D]
        in_full, back_full = g_in.whole(), g_back.whole()
        acts, slopes = [], []

        def emit(j, act_part, slope_part):
            acts.append(act_part)
            slopes.append(slope_part)

        hat, scale, low = head_up_math(
            context_all,
            picked_all,
            gains,
            out_full,
            lambda j: in_full[:, j * D : j * D + D],
            emit,
        )
        head_act = jnp.concatenate(acts, axis=1)
        hat2, scale2, final = head_down_math(hat, gains, head_act, back_full)

    other = lax.ppermute(final, "tower", [(0, 1), (1, 0)])
    if links is not None:
        column = jnp.arange(every, dtype=jnp.int32)[None]
        place_of = jnp.where(column % SLOTS == 0, column // SLOTS, -1)
        ids = jnp.repeat(dataset_ids.astype(F32), SLOTS)[None]
        columns = lambda a, width: lax.dynamic_slice(a, (0, own * width), (every, width))
        loss, d_context, d_sum, d_gains, grad_out, grad_in, grad_back = launch(
            head_back,
            [
                (asking, SMEM),
                (own.astype(jnp.int32).reshape(1), SMEM),
                (final, VMEM),
                (other, VMEM),
                (positives_all, VMEM),
                (ids, VMEM),
                (place_of, VMEM),
                (gains, VMEM),
                (hat2, VMEM),
                (scale2, VMEM),
                (hat, VMEM),
                (scale, VMEM),
                (slope, VMEM),
                (columns(head_act, back_part), VMEM),
                (columns(low, part), VMEM),
                (columns(context_all, part), VMEM),
            ],
            [g_mix, g_in, g_back],
            [
                ((8, 128), F32, VMEM),
                ((rows, SLOTS, D), F32, VMEM),
                ((rows, SLOTS, D), F32, VMEM),
                ((8, D), F32, VMEM),
                ((part, D), F32, VMEM),
                ((part, FF), F32, VMEM),
                ((back_part, D), F32, VMEM),
            ],
            [
                pltpu.VMEM((D, D), BF),
                pltpu.VMEM((D, FF), BF),
                pltpu.VMEM((FF, D), BF),
                pltpu.VMEM((every, FF), BF),
                pltpu.VMEM((every, D), F32),
                pltpu.VMEM((every, D), F32),
                sems(3, g_back.blocks),
            ],
            room=48,
            flops=2 * every * D * (2 * FF + 3 * D),
            moved=20 * MIB,
        )
        loss = loss[0, 0]
    else:
        passages = jnp.where(is_asking, other, final)[::SLOTS]
        asked = jnp.where(is_asking, final, other)
        loss, d_logits = logit_back(
            asked,
            passages,
            positives_all,
            dataset_ids.astype(F32)[None],
            jnp.arange(passages.shape[0], dtype=jnp.int32)[None],
        )
        loss = loss[0, 0]
        d_asked = dot_split(d_logits, passages)
        d_passages = dot_split(d_logits.T, asked)
        spaced = jnp.pad(d_passages[:, None], ((0, 0), (0, SLOTS - 1), (0, 0)))
        d_ups = []
        d_down, d_sum, d_att, d_context, d_gains = back_math(
            jnp.where(is_asking, d_asked, spaced.reshape(every, D)),
            hat2,
            scale2,
            hat,
            scale,
            gains,
            lambda j: slopes[j],
            lambda: out_full,
            lambda j: in_full[:, j * D : j * D + D],
            lambda j: back_full[j * D : j * D + D],
            lambda j, d_up_part: d_ups.append(d_up_part),
        )
        d_up = jnp.concatenate(d_ups, axis=1)
        d_gains = jnp.concatenate(d_gains, axis=0)
        own_rows = lambda a: lax.dynamic_slice(a, (own * heads, 0), (heads, D))
        d_sum = own_rows(d_sum).reshape(rows, SLOTS, D)
        d_context = own_rows(d_context).reshape(rows, SLOTS, D)

    if links is not None:
        z, y, x = links.at
        block = jnp.arange(devices, dtype=jnp.int32)
        far, near, line = block // 8, block // 4 % 2, (z + block) % 4 * 4
        source = jnp.stack(
            [line + (y ^ near) * 2 + (x ^ far), line + (y ^ far) * 2 + (x ^ near)]
        ).astype(jnp.int32)
        sums = [((8, part, D), BF, VMEM)] * 4
    else:
        source = jnp.zeros((2, 2), jnp.int32)
        sums = [((1, D, D), BF, VMEM)] * 4
    outs = launch(
        attend_back,
        [
            (source, SMEM),
            (q_lengths, SMEM),
            (asking, SMEM),
            (inputs, two(SEQ_LEN, D)),
            (query, two(SLOTS, D)),
            (key, two(SEQ_LEN, D)),
            (value, two(D, SEQ_LEN)),
            (d_context, two(SLOTS, D)),
        ],
        [],
        [
            ((rows, WIDE, SEQ_LEN), BF, two(WIDE, SEQ_LEN)),
            ((rows, WIDE, SEQ_LEN), BF, two(WIDE, SEQ_LEN)),
            ((rows, WIDE, D), BF, two(WIDE, D)),
            ((rows, WIDE, D), BF, two(WIDE, D)),
            ((rows, SLOTS, D), BF, two(SLOTS, D)),
        ]
        + sums,
        [
            pltpu.VMEM((2, rows * WIDE, D), BF),
            pltpu.VMEM((2, rows * WIDE, D), BF),
            pltpu.VMEM((D, D), BF),
        ],
        room=60,
        grid=(rows // 2,),
        flops=2 * rows * WIDE * D * (5 * SEQ_LEN + 2 * D),
        moved=16 * MIB,
    )
    low_probs, low_score, wide_query, wide_context, d_query = outs[:5]
    keys, keys_away, vals, vals_away = outs[5:]
    d_query_all = jnp.concatenate(gather_rows(links, d_query.reshape(heads, D), D // 2), axis=1)
    (states_grad,) = launch(
        states_back,
        [
            (low_probs, two(WIDE, SEQ_LEN)),
            (low_score, two(WIDE, SEQ_LEN)),
            (wide_query, two(WIDE, D)),
            (wide_context, two(WIDE, D)),
            (d_query, two(SLOTS, D)),
            (d_sum, two(SLOTS, D)),
        ],
        [g_mix],
        [((rows, SEQ_LEN, D), F32, two(SEQ_LEN, D))],
        [pltpu.VMEM((D, 3 * D), BF), sems(g_mix.blocks)],
        room=60,
        grid=(rows // 2,),
        flops=2 * rows * WIDE * D * (3 * D + 2 * SEQ_LEN),
        moved=12 * MIB,
    )
    if links is not None:
        key_in, val_in = move(keys_away, links.x), move(vals_away, links.y)
        keys_away, vals_away = low_sum(keys[4:], key_in[4:]), low_sum(vals[4:], val_in[4:])
        keys, vals = low_sum(keys[:4], key_in[:4]), low_sum(vals[:4], val_in[:4])
        key_in, val_in = move(keys_away, links.y), move(vals_away, links.x)
        both = jnp.stack([low_sum(keys, key_in), low_sum(vals, val_in)], axis=1)
        behind = [both]
        total = both[0].astype(F32)
        for c in (1, 2, 3):
            total = total + move(both[c], links.z[c]).astype(F32)
        grad_key, grad_val = total[0], total[1]
    else:
        grad_key = lax.psum_scatter(keys[0], "batch", scatter_dimension=0, tiled=True).astype(F32)
        grad_val = lax.psum_scatter(vals[0], "batch", scatter_dimension=0, tiled=True).astype(F32)
    (encoded,) = launch(
        down,
        [(first, two(SEQ_LEN, D)), (act, two(SEQ_LEN, FF)), (gains, VMEM)],
        [g_back],
        [((rows, SEQ_LEN, D), BF, two(SEQ_LEN, D))],
        [pltpu.VMEM((FF, D), BF), sems(g_back.blocks)],
        room=32,
        grid=(rows // 2,),
        flops=2 * rows * SEQ_LEN * D * FF,
        moved=24 * MIB,
        behind=behind,
    )
    columns = lambda a, width: lax.dynamic_slice(a, (0, own * width), (every, width))
    if links is None:
        grad_back = dot_tn(columns(head_act, back_part), d_down)
        grad_in = dot_tn(columns(low, part), d_up)
        grad_out = dot_tn(columns(context_all, part), d_att)
    grad_query = dot_tn(columns(picked_all, part), d_query_all)
    grad_qkv = jnp.concatenate([grad_query, grad_key, grad_val], axis=1)
    gain_own = lax.dynamic_slice(d_gains, (0, own * part), (4, part))
    return (
        loss,
        encoded[None],
        states_grad[None],
        grad_qkv[None],
        grad_out[None],
        grad_in[None],
        grad_back[None],
        gain_own[0:1],
        gain_own[1:2],
        gain_own[2:3],
        gain_own[3:4],
    )


def solution(mesh):
    rows = P("tower", "batch", None, None)
    matrix = P("tower", "batch", None)
    vector = P("tower", "batch")
    return jax.shard_map(
        body,
        mesh=mesh,
        in_specs=(rows, P("batch", None), P(), P("batch"))
        + (matrix,) * 4
        + (vector,) * 4,
        out_specs=(P(), rows, rows) + (matrix,) * 4 + (vector,) * 4,
        check_vma=False,
    )
```

time: 1830 us -> 320 us (0.17)
  waiting for transfers between devices: 1160 us -> 90.1 us
  blocking collectives: 231 us -> 0 us
  matrix products: 231 us -> 1.24 us
  Pallas kernels: 0 us -> 97.9 us
  local copies, waits for them, and re-layouts: 122 us -> 28.1 us
  starting transfers between devices: 23 us -> 75.5 us
  other arithmetic: 30.9 us -> 8.77 us
    unnamed x25 -> x1, waiting for transfers between devices: 585 us -> 0.68 us
    reduce_scatter x3 -> x0, waiting for transfers between devices: 483 us -> none  [the longest x1 177 us: body(): lax.psum_scatter(totals[3], 'batch', scatter_dimension=1, tiled=True)]
    dot_general x81 -> x1, matrix products: 210 us -> 1.24 us  [dot_tn(): lax.dot_general(a, b, (((0,), (0,)), ((), ())), preferred_element_type=F32)]
    unnamed x2 -> x0, blocking collectives: 115 us -> none
    pallas_call x0 -> x9, Pallas kernels: none -> 97.9 us  [launch(): pl.pallas_call(run, name=getattr(kernel, 'func', kernel).__name__, input_...]
    all_gather x4 -> x1, waiting for transfers between devices: 96.3 us -> 0.01 us  [gather_whole(): whole = lax.all_gather(shard, 'batch', axis=0, tiled=True)]
    ppermute x0 -> x52, waiting for transfers between devices: none -> 89.4 us  [the longest x51 88.9 us: move(): return lax.ppermute(value, 'batch', pairs)]
    ppermute x0 -> x52, starting transfers between devices: none -> 75.5 us  [the longest x51 75.4 us: move(): return lax.ppermute(value, 'batch', pairs)]
  transfers between devices with their start and end apart: 20 -> 53, of which waited for: 12 -> 23; matrix products, arithmetic and copies ran while one was open for 15% -> 6% of each run, Pallas kernels for 0% -> 21%
where the time goes in v1:
time: 320 us; the launch traced here: 319 us
  Pallas kernels  97.9 us (31%)
  waiting for transfers between devices  90.1 us (28%)
  starting transfers between devices  75.5 us (24%)
  local copies, waits for them, and re-layouts  28.1 us (9%)
  between operations  16.8 us (5%)
  other arithmetic  8.77 us (3%)
    pallas_call x9, Pallas kernels, launch(): pl.pallas_call(run, name=getattr(kernel, 'func', kernel).__name__, input_...  97.9 us
    ppermute x51, waiting for transfers between devices, move(): return lax.ppermute(value, 'batch', pairs)  88.9 us
    ppermute x51, starting transfers between devices, move(): return lax.ppermute(value, 'batch', pairs)  75.4 us
    unnamed x106, local copies, waits for them, and re-layouts  19.8 us
  transfers between devices with their start and end apart: 53, of which 23 were waited for; matrix products, arithmetic and copies ran while one was open for 6% of the time, Pallas kernels for 21%

profile of v1, /device:TPU:0, one launch (start us, length us, event | category | flops | bytes accessed | tf_op | source)
XLA Modules:
  0.0 318.6 jit_solution(17603834298720436393)
XLA Ops:
  10.6 4.0 %collective-permute-start.11 = (bf16[48,3200]{1,0:T(8,128)(2,1)}, bf16[48,3200]{1,0:T(8,128)(2,1)S(1)}, u32[]{:S(2)}, u32[]{:S(2)}) collective-permute-start(bf16[48,3200]{1,0:T(8,128)(2,1)} %get-tuple-element.84), channel_id=1, source_target_pairs={{0,8},{1,9},{2,10},{3,11},{4,12},{5,13},{6,14},{7,15},{8,0},{9,1},... | collective-permute-start | bytes 921608 | tf_op jit(solution)/shard_map/ppermute | solution.py:96
  16.7 21.2 %collective-permute-done.11 = bf16[48,3200]{1,0:T(8,128)(2,1)S(1)} collective-permute-done((bf16[48,3200]{1,0:T(8,128)(2,1)}, bf16[48,3200]{1,0:T(8,128)(2,1)S(1)}, u32[]{:S(2)}, u32[]{:S(2)}) %collective-permute-start.11) | collective-permute-done | bytes 307232 | tf_op jit(solution)/shard_map/ppermute | solution.py:96
  37.9 4.5 %collective-permute-start.13 = (bf16[48,3200]{1,0:T(8,128)(2,1)S(1)}, bf16[48,3200]{1,0:T(8,128)(2,1)S(1)}, u32[]{:S(2)}, u32[]{:S(2)}) collective-permute-start(bf16[48,3200]{1,0:T(8,128)(2,1)S(1)} %collective-permute-done.11), channel_id=1, source_target_pairs={{0,2},{1,3},{2,0},{3,1},{4,6},{5,7},{6,4},{7,5},{8,10},{9,11},{10,... | collective-permute-start | bytes 921608 | tf_op jit(solution)/shard_map/ppermute | solution.py:96
  46.5 4.5 %collective-permute-done.13 = bf16[48,3200]{1,0:T(8,128)(2,1)S(1)} collective-permute-done((bf16[48,3200]{1,0:T(8,128)(2,1)S(1)}, bf16[48,3200]{1,0:T(8,128)(2,1)S(1)}, u32[]{:S(2)}, u32[]{:S(2)}) %collective-permute-start.13) | collective-permute-done | bytes 307232 | tf_op jit(solution)/shard_map/ppermute | solution.py:96
  74.3 5.1 %collective-permute-start.16 = (bf16[192,768]{1,0:T(8,128)(2,1)}, bf16[192,768]{1,0:T(8,128)(2,1)}, u32[]{:S(2)}, u32[]{:S(2)}) collective-permute-start(bf16[192,768]{1,0:T(8,128)(2,1)} %get-tuple-element.89), channel_id=1, source_target_pairs={{0,12},{1,13},{2,14},{3,15},{4,0},{5,1},{6,2},{7,3},{8,4},{9,5},{1... | collective-permute-start | bytes 884744 | tf_op jit(solution)/shard_map/ppermute | solution.py:96
  83.2 9.5 %collective-permute-done.17.refs_22_ = bf16[192,768]{1,0:T(8,128)(2,1)} collective-permute-done((bf16[192,768]{1,0:T(8,128)(2,1)}, bf16[192,768]{1,0:T(8,128)(2,1)}, u32[]{:S(2)}, u32[]{:S(2)}) %collective-permute-start.17) | collective-permute-done | bytes 294944 | tf_op jit(solution)/shard_map/ppermute | solution.py:96
  100.2 9.3 %collective-permute-done.6 = bf16[48,3200]{1,0:T(8,128)(2,1)} collective-permute-done((bf16[48,3200]{1,0:T(8,128)(2,1)S(1)}, bf16[48,3200]{1,0:T(8,128)(2,1)}, u32[]{:S(2)}, u32[]{:S(2)}) %collective-permute-start.6) | collective-permute-done | bytes 307232 | tf_op jit(solution)/shard_map/ppermute | solution.py:96
  111.5 10.9 %mix.2 = (f32[6,4,768]{2,1,0:T(4,128)}, bf16[6,256,768]{2,1,0:T(8,128)(2,1)}, bf16[6,768,256]{2,1,0:T(8,128)(2,1)}, bf16[6,256,768]{2,1,0:T(8,128)(2,1)}, f32[8,768]{1,0:T(8,128)}) custom-call(s32[6,4]{1,0:T(8,128)} %copy.65.refs_0_.refs_1_, s32[1]{0:T(128)} %bitcast.refs_1_.refs_0_.refs_2_, bf16[6,256,768]{2,1,0:T(8,128)(2,1)} %bitcast.127, ...), custom_call_target="tpu_custom_call" | custom-call | flops 3925868544 | bytes 10485760 | tf_op jit(solution)/shard_map/mix/pallas_call | solution.py:212
  122.4 5.7 %collective-permute-done.22.refs_28_ = bf16[192,768]{1,0:T(8,128)(2,1)} collective-permute-done((bf16[192,768]{1,0:T(8,128)(2,1)}, bf16[192,768]{1,0:T(8,128)(2,1)}, u32[]{:S(2)}, u32[]{:S(2)}) %collective-permute-start.22) | collective-permute-done | bytes 294944 | tf_op jit(solution)/shard_map/ppermute | solution.py:96
  131.3 10.8 %mix.3 = (f32[6,4,768]{2,1,0:T(4,128)}, bf16[6,256,768]{2,1,0:T(8,128)(2,1)}, bf16[6,768,256]{2,1,0:T(8,128)(2,1)}, bf16[6,256,768]{2,1,0:T(8,128)(2,1)}) custom-call(s32[6,4]{1,0:T(8,128)} %copy.65.refs_0_.refs_1_, s32[1]{0:T(128)} %bitcast.refs_1_.refs_0_.refs_2_, ...), custom_call_target="tpu_custom_call", output_to_operand_aliasing={{0}: (3, {}), {1}: (4, {}), {2}: (5, {}), {3}: (6, {})} | custom-call | flops 3925868544 | bytes 10485760 | tf_op jit(solution)/shard_map/mix/pallas_call | solution.py:212
  143.3 7.5 %collective-permute-start.24 = (bf16[24,1664]{1,0:T(8,128)(2,1)S(1)}, bf16[24,1664]{1,0:T(8,128)(2,1)S(1)}, u32[]{:S(2)}, u32[]{:S(2)}) collective-permute-start(bf16[24,1664]{1,0:T(8,128)(2,1)S(1)} %fusion.24), channel_id=1, source_target_pairs={{0,12},{1,13},{2,14},{3,15},{4,0},{5,1},{6,2},{7,3},{8,4},{9,5},{1... | collective-permute-start | bytes 239624 | tf_op jit(solution)/shard_map/ppermute | solution.py:96
  154.6 6.8 %collective-permute-done.25 = bf16[24,1664]{1,0:T(8,128)(2,1)S(1)} collective-permute-done((bf16[24,1664]{1,0:T(8,128)(2,1)S(1)}, bf16[24,1664]{1,0:T(8,128)(2,1)S(1)}, u32[]{:S(2)}, u32[]{:S(2)}) %collective-permute-start.25) | collective-permute-done | bytes 79904 | tf_op jit(solution)/shard_map/ppermute | solution.py:96
  168.4 3.2 collective-permute-done.29
  172.3 4.1 %collective-permute-done.28 = bf16[2,96,768]{2,1,0:T(8,128)(2,1)S(1)} collective-permute-done((bf16[2,96,768]{2,1,0:T(8,128)(2,1)S(1)}, bf16[2,96,768]{2,1,0:T(8,128)(2,1)S(1)}, u32[]{:S(2)}, u32[]{:S(2)}) %collective-permute-start.28) | collective-permute-done | bytes 294944 | tf_op jit(solution)/shard_map/ppermute | solution.py:96
  192.4 17.9 %up.1 = (bf16[6,256,768]{2,1,0:T(8,128)(2,1)S(1)}, bf16[6,256,3072]{2,1,0:T(8,128)(2,1)}) custom-call(bf16[6,256,768]{2,1,0:T(8,128)(2,1)S(1)} %bitcast.130, bf16[6,256,768]{2,1,0:T(8,128)(2,1)S(1)} %copy-done.30, f32[8,768]{1,0:T(8,128)S(1)} %copy-done.35, s32[16]{0:T(128)S(1)} %copy-done.38, bf16[1,48,3200]{2,1,0:T(8,128)(2,1)S(1)} %copy-done.3, ...), custom_call_target="tpu_custom_call" | custom-call | flops 9059696640 | bytes 31457280 | tf_op jit(solution)/shard_map/up/pallas_call | solution.py:212
  211.7 6.2 %head_up.1 = (f32[384,768]{1,0:T(8,128)S(1)}, f32[384,128]{1,0:T(8,128)S(1)}, bf16[384,768]{1,0:T(8,128)(2,1)S(1)}, bf16[384,3072]{1,0:T(8,128)(2,1)S(1)}, bf16[384,3072]{1,0:T(8,128)(2,1)S(1)}) custom-call(bf16[384,768]{1,0:T(8,128)(2,1)S(1)} %bitcast.192, bf16[384,768]{1,0:T(8,128)(2,1)S(1)} %copy-done.31, f32[8,768]{1,0:T(8,128)S(1)} %copy-done.35, ...), custom_call_target="tpu_custom_call" | custom-call | flops 2264924160 | bytes 14680064 | tf_op jit(solution)/shard_map/head_up/pallas_call | solution.py:212
  218.0 5.8 %head_down.1 = (f32[384,768]{1,0:T(8,128)S(1)}, f32[384,128]{1,0:T(8,128)S(1)}, bf16[384,768]{1,0:T(8,128)(2,1)S(1)}) custom-call(f32[384,768]{1,0:T(8,128)S(1)} %get-tuple-element.53.refs_0_.refs_10_, bf16[384,3072]{1,0:T(8,128)(2,1)S(1)} %get-tuple-element.54.refs_1_, f32[8,768]{1,0:T(8,128)S(1)} %copy-done.35, s32[16]{0:T(128)S(1)} %copy-done.38, ...), custom_call_target="tpu_custom_call" | custom-call | flops 1811939328 | bytes 10485760 | tf_op jit(solution)/shard_map/head_down/pallas_call | solution.py:212
  226.8 15.3 %head_back.1 = (f32[8,128]{1,0:T(8,128)S(1)}, f32[6,4,768]{2,1,0:T(4,128)S(1)}, f32[6,4,768]{2,1,0:T(4,128)S(1)}, f32[8,768]{1,0:T(8,128)S(1)}, f32[48,768]{1,0:...) custom-call(s32[1]{0:T(128)} %bitcast.refs_1_.refs_0_.refs_2_, s32[1]{0:T(128)} %bitcast.1.refs_1_, ...), custom_call_target="tpu_custom_call" | custom-call | flops 4982833152 | bytes 20971520 | tf_op jit(solution)/shard_map/head_back/pallas_call | solution.py:212
  243.4 8.9 %attend_back.1 = (bf16[6,48,256]{2,1,0:T(8,128)(2,1)}, bf16[6,48,256]{2,1,0:T(8,128)(2,1)}, bf16[6,48,768]{2,1,0:T(8,128)(2,1)}, bf16[6,48,768]{2,1,0:T(8,128)(2...) custom-call(s32[2,16]{1,0:T(2,128)} %pad_add_fusion.refs_0_, ...), custom_call_target="tpu_custom_call" | custom-call | flops 1245708288 | bytes 16777216 | tf_op jit(solution)/shard_map/attend_back/pallas_call | solution.py:212
  260.8 9.1 %states_back.1 = f32[6,256,768]{2,1,0:T(8,128)} custom-call(bf16[6,48,256]{2,1,0:T(8,128)(2,1)} %get-tuple-element.71.refs_0_, bf16[6,48,256]{2,1,0:T(8,128)(2,1)} %get-tuple-element.72.refs_1_, bf16[6,48,768]{2,1,0:T(8,128)(2,1)} %get-tuple-element.73.refs_2_, bf16[6,48,768]{2,1,0:T(8,128)(2,1)} %get-tuple-element.74.refs_3_, ...), custom_call_target="tpu_custom_call" | custom-call | flops 1245708288 | bytes 12582912 | tf_op jit(solution)/shard_map/states_back/pallas_call | solution.py:212
  276.5 3.3 %collective-permute-done.46 = bf16[2,96,384]{2,1,0:T(8,128)(2,1)S(1)} collective-permute-done((bf16[2,96,384]{2,1,0:T(8,128)(2,1)S(1)}, bf16[2,96,384]{2,1,0:T(8,128)(2,1)S(1)}, u32[]{:S(2)}, u32[]{:S(2)}) %collective-permute-start.46) | collective-permute-done | bytes 147488 | tf_op jit(solution)/shard_map/ppermute | solution.py:96
  284.3 3.2 %collective-permute-done.39 = bf16[4,48,768]{2,1,0:T(8,128)(2,1)S(1)} collective-permute-done((bf16[4,48,768]{2,1,0:T(8,128)(2,1)S(1)}, bf16[4,48,768]{2,1,0:T(8,128)(2,1)S(1)}, u32[]{:S(2)}, u32[]{:S(2)}) %collective-permute-start.39) | collective-permute-done | bytes 294944 | tf_op jit(solution)/shard_map/ppermute | solution.py:96
  294.1 3.7 %copy-done.2 = bf16[6,256,3072]{2,1,0:T(8,128)(2,1)S(1)} copy-done((bf16[6,256,3072]{2,1,0:T(8,128)(2,1)S(1)}, bf16[6,256,3072]{2,1,0:T(8,128)(2,1)}, u32[]{:S(2)}) %copy-start.2) | copy-done | bytes 9437208
  297.8 13.0 %down.1 = bf16[6,256,768]{2,1,0:T(8,128)(2,1)} custom-call(bf16[6,256,768]{2,1,0:T(8,128)(2,1)S(1)} %copy-done.41, bf16[6,256,3072]{2,1,0:T(8,128)(2,1)S(1)} %copy-done.2, f32[8,768]{1,0:T(8,128)S(1)} %copy-done.35, s32[16]{0:T(128)S(1)} %copy-done.39, bf16[1,192,768]{2,1,0:T(8,128)(2,1)} %get-tuple-element.88.refs_4_.refs_36_, ...), custom_call_target="tpu_custom_call" | custom-call | flops 7247757312 | bytes 25165824 | tf_op jit(solution)/shard_map/down/pallas_call | solution.py:212
  (264 shorter events, 108.3 us)
Async XLA Ops:
  7.2 175.7 %all-gather.3.cloned.1.call-start = ((), (), s32[]{:S(2)}) async-start(), calls=%async_computation | async-start | bytes 5013504 | tf_op jit(solution)/shard_map/all_gather | solution.py:138
  10.6 27.3 %collective-permute-start.11 = (bf16[48,3200]{1,0:T(8,128)(2,1)}, bf16[48,3200]{1,0:T(8,128)(2,1)S(1)}, u32[]{:S(2)}, u32[]{:S(2)}) collective-permute-start(bf16[48,3200]{1,0:T(8,128)(2,1)} %get-tuple-element.84), channel_id=1, source_target_pairs={{0,8},{1,9},{2,10},{3,11},{4,12},{5,13},{6,14},{7,15},{8,0},{9,1},... | collective-permute-start | bytes 921608 | tf_op jit(solution)/shard_map/ppermute | solution.py:96
  14.7 29.6 %collective-permute-start.7 = (bf16[48,3200]{1,0:T(8,128)(2,1)}, bf16[48,3200]{1,0:T(8,128)(2,1)S(1)}, u32[]{:S(2)}, u32[]{:S(2)}) collective-permute-start(bf16[48,3200]{1,0:T(8,128)(2,1)} %get-tuple-element.84), channel_id=1, source_target_pairs={{0,12},{1,13},{2,14},{3,15},{4,0},{5,1},{6,2},{7,3},{8,4},{9,5},{1... | collective-permute-start | bytes 921608 | tf_op jit(solution)/shard_map/ppermute | solution.py:96
  16.0 28.5 %collective-permute-start.3 = (bf16[48,3200]{1,0:T(8,128)(2,1)}, bf16[48,3200]{1,0:T(8,128)(2,1)S(1)}, u32[]{:S(2)}, u32[]{:S(2)}) collective-permute-start(bf16[48,3200]{1,0:T(8,128)(2,1)} %get-tuple-element.84), channel_id=1, source_target_pairs={{0,4},{1,5},{2,6},{3,7},{4,8},{5,9},{6,10},{7,11},{8,12},{9,13},{1... | collective-permute-start | bytes 921608 | tf_op jit(solution)/shard_map/ppermute | solution.py:96
  44.2 21.9 %collective-permute-start = (bf16[48,3200]{1,0:T(8,128)(2,1)}, bf16[48,3200]{1,0:T(8,128)(2,1)S(1)}, u32[]{:S(2)}, u32[]{:S(2)}) collective-permute-start(bf16[48,3200]{1,0:T(8,128)(2,1)} %get-tuple-element.84), channel_id=1, source_target_pairs={{0,1},{1,0},{2,3},{3,2},{4,5},{5,4},{6,7},{7,6},{8,9},{9,8},{10,11... | collective-permute-start | bytes 921608 | tf_op jit(solution)/shard_map/ppermute | solution.py:96
  44.5 23.2 %collective-permute-start.9 = (bf16[48,3200]{1,0:T(8,128)(2,1)S(1)}, bf16[48,3200]{1,0:T(8,128)(2,1)S(1)}, u32[]{:S(2)}, u32[]{:S(2)}) collective-permute-start(bf16[48,3200]{1,0:T(8,128)(2,1)S(1)} %collective-permute-done.7), channel_id=1, source_target_pairs={{0,2},{1,3},{2,0},{3,1},{4,6},{5,7},{6,4},{7,5},{8,10},{9,11},{10,... | collective-permute-start | bytes 921608 | tf_op jit(solution)/shard_map/ppermute | solution.py:96
  50.9 19.3 %collective-permute-start.8 = (bf16[48,3200]{1,0:T(8,128)(2,1)S(1)}, bf16[48,3200]{1,0:T(8,128)(2,1)S(1)}, u32[]{:S(2)}, u32[]{:S(2)}) collective-permute-start(bf16[48,3200]{1,0:T(8,128)(2,1)S(1)} %collective-permute-done.7), channel_id=1, source_target_pairs={{0,1},{1,0},{2,3},{3,2},{4,5},{5,4},{6,7},{7,6},{8,9},{9,8},{10,11... | collective-permute-start | bytes 921608 | tf_op jit(solution)/shard_map/ppermute | solution.py:96
  70.2 22.5 %collective-permute-start.17 = (bf16[192,768]{1,0:T(8,128)(2,1)}, bf16[192,768]{1,0:T(8,128)(2,1)}, u32[]{:S(2)}, u32[]{:S(2)}) collective-permute-start(bf16[192,768]{1,0:T(8,128)(2,1)} %get-tuple-element.89), channel_id=1, source_target_pairs={{0,8},{1,9},{2,10},{3,11},{4,12},{5,13},{6,14},{7,15},{8,0},{9,1},... | collective-permute-start | bytes 884744 | tf_op jit(solution)/shard_map/ppermute | solution.py:96
  74.3 20.5 %collective-permute-start.16 = (bf16[192,768]{1,0:T(8,128)(2,1)}, bf16[192,768]{1,0:T(8,128)(2,1)}, u32[]{:S(2)}, u32[]{:S(2)}) collective-permute-start(bf16[192,768]{1,0:T(8,128)(2,1)} %get-tuple-element.89), channel_id=1, source_target_pairs={{0,12},{1,13},{2,14},{3,15},{4,0},{5,1},{6,2},{7,3},{8,4},{9,5},{1... | collective-permute-start | bytes 884744 | tf_op jit(solution)/shard_map/ppermute | solution.py:96
  81.2 28.3 %collective-permute-start.14 = (bf16[48,3200]{1,0:T(8,128)(2,1)S(1)}, bf16[48,3200]{1,0:T(8,128)(2,1)}, u32[]{:S(2)}, u32[]{:S(2)}) collective-permute-start(bf16[48,3200]{1,0:T(8,128)(2,1)S(1)} %collective-permute-done.13), channel_id=1, source_target_pairs={{0,1},{1,0},{2,3},{3,2},{4,5},{5,4},{6,7},{7,6},{8,9},{9,8},{10,11... | collective-permute-start | bytes 921608 | tf_op jit(solution)/shard_map/ppermute | solution.py:96
  94.8 27.6 %collective-permute-start.18 = (bf16[192,768]{1,0:T(8,128)(2,1)}, bf16[192,768]{1,0:T(8,128)(2,1)S(1)}, u32[]{:S(2)}, u32[]{:S(2)}) collective-permute-start(bf16[192,768]{1,0:T(8,128)(2,1)} %bitcast.41), channel_id=1, source_target_pairs={{0,1},{1,0},{2,3},{3,2},{4,5},{5,4},{6,7},{7,6},{8,9},{9,8},{10,11... | collective-permute-start | bytes 884744 | tf_op jit(solution)/shard_map/ppermute | solution.py:96
  98.6 23.8 %collective-permute-start.23 = (bf16[192,768]{1,0:T(8,128)(2,1)}, bf16[192,768]{1,0:T(8,128)(2,1)}, u32[]{:S(2)}, u32[]{:S(2)}) collective-permute-start(bf16[192,768]{1,0:T(8,128)(2,1)} %collective-permute-done.16.refs_21_), channel_id=1, source_target_pairs={{0,2},{1,3},{2,0},{3,1},{4,6},{5,7},{6,4},{7,5},{8,10},{9,11},{10,... | collective-permute-start | bytes 884744 | tf_op jit(solution)/shard_map/ppermute | solution.py:96
  100.2 27.9 %collective-permute-start.22 = (bf16[192,768]{1,0:T(8,128)(2,1)}, bf16[192,768]{1,0:T(8,128)(2,1)}, u32[]{:S(2)}, u32[]{:S(2)}) collective-permute-start(bf16[192,768]{1,0:T(8,128)(2,1)} %collective-permute-done.16.refs_21_), channel_id=1, source_target_pairs={{0,1},{1,0},{2,3},{3,2},{4,5},{5,4},{6,7},{7,6},{8,9},{9,8},{10,11... | collective-permute-start | bytes 884744 | tf_op jit(solution)/shard_map/ppermute | solution.py:96
  109.5 21.8 %collective-permute-start.20 = (bf16[192,768]{1,0:T(8,128)(2,1)}, bf16[192,768]{1,0:T(8,128)(2,1)}, u32[]{:S(2)}, u32[]{:S(2)}) collective-permute-start(bf16[192,768]{1,0:T(8,128)(2,1)} %collective-permute-done.15.refs_20_), channel_id=1, source_target_pairs={{0,1},{1,0},{2,3},{3,2},{4,5},{5,4},{6,7},{7,6},{8,9},{9,8},{10,11... | collective-permute-start | bytes 884744 | tf_op jit(solution)/shard_map/ppermute | solution.py:96
  151.4 66.5 %collective-permute-start.31 = (bf16[192,768]{1,0:T(8,128)(2,1)}, bf16[192,768]{1,0:T(8,128)(2,1)}, u32[]{:S(2)}, u32[]{:S(2)}) collective-permute-start(bf16[192,768]{1,0:T(8,128)(2,1)} %copy-done.28), channel_id=1, source_target_pairs={{0,2},{1,3},{2,0},{3,1},{4,6},{5,7},{6,4},{7,5},{8,10},{9,11},{10,... | collective-permute-start | bytes 884744 | tf_op jit(solution)/shard_map/ppermute | solution.py:96
  152.9 26.1 %collective-permute-start.35 = (bf16[192,768]{1,0:T(8,128)(2,1)}, bf16[192,768]{1,0:T(8,128)(2,1)}, u32[]{:S(2)}, u32[]{:S(2)}) collective-permute-start(bf16[192,768]{1,0:T(8,128)(2,1)} %collective-permute-done.17.refs_22_), channel_id=1, source_target_pairs={{0,2},{1,3},{2,0},{3,1},{4,6},{5,7},{6,4},{7,5},{8,10},{9,11},{10,... | collective-permute-start | bytes 884744 | tf_op jit(solution)/shard_map/ppermute | solution.py:96
  153.4 64.5 %collective-permute-start.34 = (bf16[192,768]{1,0:T(8,128)(2,1)}, bf16[192,768]{1,0:T(8,128)(2,1)}, u32[]{:S(2)}, u32[]{:S(2)}) collective-permute-start(bf16[192,768]{1,0:T(8,128)(2,1)} %collective-permute-done.17.refs_22_), channel_id=1, source_target_pairs={{0,1},{1,0},{2,3},{3,2},{4,5},{5,4},{6,7},{7,6},{8,9},{9,8},{10,11... | collective-permute-start | bytes 884744 | tf_op jit(solution)/shard_map/ppermute | solution.py:96
  176.4 41.6 %collective-permute-start.33 = (bf16[192,768]{1,0:T(8,128)(2,1)}, bf16[192,768]{1,0:T(8,128)(2,1)}, u32[]{:S(2)}, u32[]{:S(2)}) collective-permute-start(bf16[192,768]{1,0:T(8,128)(2,1)} %collective-permute-done.22.refs_28_), channel_id=1, source_target_pairs={{0,2},{1,3},{2,0},{3,1},{4,6},{5,7},{6,4},{7,5},{8,10},{9,11},{10,... | collective-permute-start | bytes 884744 | tf_op jit(solution)/shard_map/ppermute | solution.py:96
  179.0 39.0 %collective-permute-start.32 = (bf16[192,768]{1,0:T(8,128)(2,1)}, bf16[192,768]{1,0:T(8,128)(2,1)}, u32[]{:S(2)}, u32[]{:S(2)}) collective-permute-start(bf16[192,768]{1,0:T(8,128)(2,1)} %collective-permute-done.21.refs_27_), channel_id=1, source_target_pairs={{0,1},{1,0},{2,3},{3,2},{4,5},{5,4},{6,7},{7,6},{8,9},{9,8},{10,11... | collective-permute-start | bytes 884744 | tf_op jit(solution)/shard_map/ppermute | solution.py:96
  179.6 38.3 %collective-permute-start.36 = (bf16[192,768]{1,0:T(8,128)(2,1)}, bf16[192,768]{1,0:T(8,128)(2,1)}, u32[]{:S(2)}, u32[]{:S(2)}) collective-permute-start(bf16[192,768]{1,0:T(8,128)(2,1)} %collective-permute-done.35), channel_id=1, source_target_pairs={{0,1},{1,0},{2,3},{3,2},{4,5},{5,4},{6,7},{7,6},{8,9},{9,8},{10,11... | collective-permute-start | bytes 884744 | tf_op jit(solution)/shard_map/ppermute | solution.py:96
  258.0 22.6 %collective-permute-start.38 = (bf16[8,48,768]{2,1,0:T(8,128)(2,1)}, bf16[8,48,768]{2,1,0:T(8,128)(2,1)S(1)}, u32[]{:S(2)}, u32[]{:S(2)}) collective-permute-start(bf16[8,48,768]{2,1,0:T(8,128)(2,1)} %get-tuple-element.68), channel_id=1, source_target_pairs={{0,1},{1,0},{2,3},{3,2},{4,5},{5,4},{6,7},{7,6},{8,9},{9,8},{10,11... | collective-permute-start | bytes 1769480 | tf_op jit(solution)/shard_map/ppermute | solution.py:96
  258.7 23.6 %collective-permute-start.40 = (bf16[8,48,768]{2,1,0:T(8,128)(2,1)}, bf16[8,48,768]{2,1,0:T(8,128)(2,1)S(1)}, u32[]{:S(2)}, u32[]{:S(2)}) collective-permute-start(bf16[8,48,768]{2,1,0:T(8,128)(2,1)} %get-tuple-element.70), channel_id=1, source_target_pairs={{0,2},{1,3},{2,0},{3,1},{4,6},{5,7},{6,4},{7,5},{8,10},{9,11},{10,... | collective-permute-start | bytes 1769480 | tf_op jit(solution)/shard_map/ppermute | solution.py:96
  289.4 21.4 %collective-permute-start.49 = (bf16[2,48,768]{2,1,0:T(8,128)(2,1)S(1)}, bf16[2,48,768]{2,1,0:T(8,128)(2,1)S(1)}, u32[]{:S(2)}, u32[]{:S(2)}) collective-permute-start(bf16[2,48,768]{2,1,0:T(8,128)(2,1)S(1)} %get-tuple-element.81), channel_id=1, source_target_pairs={{0,4},{1,5},{2,6},{3,7},{4,8},{5,9},{6,10},{7,11},{8,12},{9,13},{1... | collective-permute-start | bytes 442376 | tf_op jit(solution)/shard_map/ppermute | solution.py:96
  290.0 20.8 %collective-permute-start.50 = (bf16[2,48,768]{2,1,0:T(8,128)(2,1)S(1)}, bf16[2,48,768]{2,1,0:T(8,128)(2,1)S(1)}, u32[]{:S(2)}, u32[]{:S(2)}) collective-permute-start(bf16[2,48,768]{2,1,0:T(8,128)(2,1)S(1)} %get-tuple-element.82), channel_id=1, source_target_pairs={{0,8},{1,9},{2,10},{3,11},{4,12},{5,13},{6,14},{7,15},{8,0},{9,1},... | collective-permute-start | bytes 442376 | tf_op jit(solution)/shard_map/ppermute | solution.py:96
  (76 other events, 1129.1 us)
Sparse Core Ops, SparseCore 0:
  10.8 124.3 all-gather.2
